TPU v7x, 32 devices: a whole 2x2x4 slice. The times are simulated.
32 devices in a mesh: groups: 2 (over x), node: 16 (over z, y, core).
Axes of the slice: x: 2, y: 2, z: 4, core: 2. Of those that a mesh axis runs over, the one named last changes fastest.
Arguments:
- features: bfloat16 [262144, 128], P(('groups', 'node')), parts along dimension 0, may hold values from -6 to 6
- neighbors: int32 [262144, 16], P(('groups', 'node')), parts along dimension 0, may hold values from 0 to 10367
- degree: int32 [262144], P(('groups', 'node')), parts along dimension 0, may hold values from 1 to 16
- send_list: int32 [32, 16, 128], P(('groups', 'node')), parts along dimension 0, may hold values from 0 to 8191
- hub_rows: int32 [32, 8], P(('groups', 'node')), parts along dimension 0, may hold values from 0 to 8191
- w_self: bfloat16 [128, 128], replicated, may hold values from -0.5 to 0.5
- w_neigh: bfloat16 [128, 128], replicated, may hold values from -0.5 to 0.5
- bias: float32 [128], replicated, may hold values from -3 to 3
Outputs:
- hidden_out: bfloat16 [262144, 128], P(('groups', 'node')), parts along dimension 0
There are 2 independent parts, one for each index of `groups`. A program takes and returns all parts, laid end to end along the dimension named above; an argument that names none is the same for every part. Nothing has to cross between parts.
All inputs are finite; a program needn't handle non-finite values.
Results may differ from a plain program's by a relative error of at most 0.0026.
Values may be sent and summed in bfloat16 or wider, within the bound.
No kernel may reach another device: no remote copies, remote signals or barrier semaphores. Data moves between devices by JAX's collectives and lax.ppermute only.
A program may use at most 128 MiB of HBM per device.

v0:
```python
import jax
import jax.numpy as jnp
from jax import lax
from jax.sharding import PartitionSpec as P


def local(features, neighbors, degree, send_list, hub_rows, w_self, w_neigh, bias):
    width = features.shape[1]
    outgoing = jnp.take(features, send_list[0], axis=0)
    mine = jnp.take(features, hub_rows[0], axis=0)
    halo = lax.all_to_all(outgoing, "node", split_axis=0, concat_axis=0, tiled=True).reshape(
        -1, width
    )
    hubs = lax.all_gather(mine, "node", axis=0, tiled=True)
    table = jnp.concatenate([features, halo, hubs], axis=0)
    local_rows = neighbors.shape[0]
    fanout = neighbors.shape[1]
    total = jnp.zeros((local_rows, width), jnp.float32)
    for slot in range(fanout):
        picked = jnp.take(table, neighbors[:, slot], axis=0).astype(jnp.float32)
        total = total + jnp.where(degree[:, None] > slot, picked, 0.0)
    aggregate = (total / degree[:, None].astype(jnp.float32)).astype(jnp.bfloat16)
    mixed = jnp.dot(features, w_self, preferred_element_type=jnp.float32)
    mixed = mixed + jnp.dot(aggregate, w_neigh, preferred_element_type=jnp.float32) + bias
    return jnp.maximum(mixed, 0.0).astype(jnp.bfloat16)


def solution(mesh):
    in_specs = (
        P(("groups", "node"), None),
        P(("groups", "node"), None),
        P(("groups", "node")),
        P(("groups", "node"), None, None),
        P(("groups", "node"), None),
        P(),
        P(),
        P(),
    )
    out_specs = P(("groups", "node"), None)
    return jax.shard_map(local, mesh=mesh, in_specs=in_specs, out_specs=out_specs, check_vma=False)
```

profile of v0, /device:TPU:0, one launch (start us, length us, event | category | flops | bytes accessed | tf_op | source)
XLA Modules:
  0.0 591.6 jit_solution(15945647754872269162)
XLA Ops:
  0.0 0.7 compare_and_fusion.16
  0.7 0.7 fusion.21
  1.4 7.5 %gather_fusion = bf16[2048,128]{1,0:T(8,128)(2,1)S(1)} fusion(bf16[8192,128]{1,0:T(8,128)(2,1)} %param.10, s32[2048]{0:T(1024)S(1)} %fusion.21), kind=kCustom, calls=%fused_computation.16 | custom fusion | bytes 1056768 | tf_op jit(solution)/shard_map/jit(_take)/gather | solution.py:9
  8.9 0.0 copy-start.40
  8.9 0.0 copy-start.1
  8.9 1.1 broadcast_select_fusion
  10.0 7.5 %all-to-all-start = ((bf16[16,128,128]{2,1,0:T(8,128)(2,1)}), bf16[16,128,128]{2,1,0:T(8,128)(2,1)S(1)}, u32[]{:S(2)}, u32[]{:S(2)}) async-start(bf16[16,128,128]{2,1,0:T(8,128)(2,1)} %broadcast_select_fusion), calls=%async_computation | async-start | bytes 1048576 | tf_op jit(solution)/shard_map/all_to_all | solution.py:11
  17.6 0.5 compare_and_fusion.17
  18.1 3.4 fusion.25
  21.6 0.6 compare_and_fusion.14
  22.2 0.6 compare_and_fusion.4
  22.9 0.6 compare_and_fusion.6
  23.5 0.6 compare_and_fusion.8
  24.2 0.6 fusion.11
  24.8 0.6 compare_and_fusion.10
  25.4 0.6 fusion.9
  26.0 0.6 fusion.6
  26.6 0.6 compare_and_fusion.12
  27.3 0.6 fusion.7
  27.9 0.6 gather_fusion.1
  28.4 0.7 broadcast_select_fusion.1
  29.1 22.9 %all_gather.3 = bf16[128,128]{1,0:T(8,128)(2,1)} all-gather(bf16[8,128]{1,0:T(8,128)(2,1)S(1)} %broadcast_select_fusion.1), channel_id=1, replica_groups=mesh['groups'=2,'node'=16] {'node'}, dimensions={0}, use_global_device_ids=true | all-gather | bytes 34816 | tf_op jit(solution)/shard_map/all_gather | solution.py:14
  52.0 0.6 convert_element_type.74
  52.6 0.6 fusion.18
  53.2 0.6 fusion.19
  53.8 0.6 compare_and_fusion
  54.4 0.7 broadcast_compare_fusion.15
  55.1 2.7 fusion.26
  57.8 7.2 %pad_maximum_fusion = bf16[10368,128]{1,0:T(8,128)(2,1)S(1)} fusion(bf16[128,128]{1,0:T(8,128)(2,1)} %all_gather.3, bf16[2048,128]{1,0:T(8,128)(2,1)S(1)} %bitcast.39, bf16[8192,128]{1,0:T(8,128)(2,1)} %param.10), kind=kLoop, calls=%fused_computation.23 | loop fusion | flops 7962624 | bytes 5308416 | tf_op jit(solution)/shard_map/concatenate | solution.py:15
  65.0 31.9 %gather_fusion.17 = bf16[8192,128]{1,0:T(8,128)(2,1)} fusion(bf16[10368,128]{1,0:T(8,128)(2,1)S(1)} %pad_maximum_fusion, s32[8192]{0:T(1024)} %fusion.19), kind=kCustom, calls=%fused_computation.15.clone | custom fusion | bytes 4227072 | tf_op jit(solution)/shard_map/jit(_take)/gather | solution.py:20
  96.9 29.2 %gather_fusion.16 = bf16[8192,128]{1,0:T(8,128)(2,1)} fusion(bf16[10368,128]{1,0:T(8,128)(2,1)S(1)} %pad_maximum_fusion, s32[8192]{0:T(1024)S(1)} %copy-done.6), kind=kCustom, calls=%fused_computation.14.clone | custom fusion | bytes 4227072 | tf_op jit(solution)/shard_map/jit(_take)/gather | solution.py:20
  126.1 29.2 %gather_fusion.15 = bf16[8192,128]{1,0:T(8,128)(2,1)} fusion(bf16[10368,128]{1,0:T(8,128)(2,1)S(1)} %pad_maximum_fusion, s32[8192]{0:T(1024)S(1)} %fusion.17), kind=kCustom, calls=%fused_computation.13.clone | custom fusion | bytes 4227072 | tf_op jit(solution)/shard_map/jit(_take)/gather | solution.py:20
  155.3 29.2 %gather_fusion.14 = bf16[8192,128]{1,0:T(8,128)(2,1)} fusion(bf16[10368,128]{1,0:T(8,128)(2,1)S(1)} %pad_maximum_fusion, s32[8192]{0:T(1024)S(1)} %fusion.16), kind=kCustom, calls=%fused_computation.12.clone | custom fusion | bytes 4227072 | tf_op jit(solution)/shard_map/jit(_take)/gather | solution.py:20
  184.5 29.2 %gather_fusion.13 = bf16[8192,128]{1,0:T(8,128)(2,1)} fusion(bf16[10368,128]{1,0:T(8,128)(2,1)S(1)} %pad_maximum_fusion, s32[8192]{0:T(1024)S(1)} %fusion.15), kind=kCustom, calls=%fused_computation.11.clone | custom fusion | bytes 4227072 | tf_op jit(solution)/shard_map/jit(_take)/gather | solution.py:20
  213.7 29.2 %gather_fusion.12 = bf16[8192,128]{1,0:T(8,128)(2,1)} fusion(bf16[10368,128]{1,0:T(8,128)(2,1)S(1)} %pad_maximum_fusion, s32[8192]{0:T(1024)S(1)} %fusion.14), kind=kCustom, calls=%fused_computation.10.clone | custom fusion | bytes 4227072 | tf_op jit(solution)/shard_map/jit(_take)/gather | solution.py:20
  242.9 29.2 %gather_fusion.11 = bf16[8192,128]{1,0:T(8,128)(2,1)} fusion(bf16[10368,128]{1,0:T(8,128)(2,1)S(1)} %pad_maximum_fusion, s32[8192]{0:T(1024)S(1)} %fusion.13), kind=kCustom, calls=%fused_computation.9.clone | custom fusion | bytes 4227072 | tf_op jit(solution)/shard_map/jit(_take)/gather | solution.py:20
  272.1 29.2 %gather_fusion.10 = bf16[8192,128]{1,0:T(8,128)(2,1)} fusion(bf16[10368,128]{1,0:T(8,128)(2,1)S(1)} %pad_maximum_fusion, s32[8192]{0:T(1024)S(1)} %fusion.12), kind=kCustom, calls=%fused_computation.8.clone | custom fusion | bytes 4227072 | tf_op jit(solution)/shard_map/jit(_take)/gather | solution.py:20
  301.3 29.2 %gather_fusion.9 = bf16[8192,128]{1,0:T(8,128)(2,1)} fusion(bf16[10368,128]{1,0:T(8,128)(2,1)S(1)} %pad_maximum_fusion, s32[8192]{0:T(1024)S(1)} %copy-done.3), kind=kCustom, calls=%fused_computation.7.clone | custom fusion | bytes 4227072 | tf_op jit(solution)/shard_map/jit(_take)/gather | solution.py:20
  330.5 29.2 %gather_fusion.8 = bf16[8192,128]{1,0:T(8,128)(2,1)} fusion(bf16[10368,128]{1,0:T(8,128)(2,1)S(1)} %pad_maximum_fusion, s32[8192]{0:T(1024)S(1)} %fusion.10), kind=kCustom, calls=%fused_computation.6.clone | custom fusion | bytes 4227072 | tf_op jit(solution)/shard_map/jit(_take)/gather | solution.py:20
  359.7 29.2 %gather_fusion.7 = bf16[8192,128]{1,0:T(8,128)(2,1)} fusion(bf16[10368,128]{1,0:T(8,128)(2,1)S(1)} %pad_maximum_fusion, s32[8192]{0:T(1024)S(1)} %copy-done.4), kind=kCustom, calls=%fused_computation.5.clone | custom fusion | bytes 4227072 | tf_op jit(solution)/shard_map/jit(_take)/gather | solution.py:20
  388.9 29.2 %gather_fusion.6 = bf16[8192,128]{1,0:T(8,128)(2,1)} fusion(bf16[10368,128]{1,0:T(8,128)(2,1)S(1)} %pad_maximum_fusion, s32[8192]{0:T(1024)S(1)} %fusion.8), kind=kCustom, calls=%fused_computation.4.clone | custom fusion | bytes 4227072 | tf_op jit(solution)/shard_map/jit(_take)/gather | solution.py:20
  418.1 29.2 %gather_fusion.5 = bf16[8192,128]{1,0:T(8,128)(2,1)} fusion(bf16[10368,128]{1,0:T(8,128)(2,1)S(1)} %pad_maximum_fusion, s32[8192]{0:T(1024)S(1)} %copy-done.5), kind=kCustom, calls=%fused_computation.3.clone | custom fusion | bytes 4227072 | tf_op jit(solution)/shard_map/jit(_take)/gather | solution.py:20
  447.3 29.2 %gather_fusion.4 = bf16[8192,128]{1,0:T(8,128)(2,1)} fusion(bf16[10368,128]{1,0:T(8,128)(2,1)S(1)} %pad_maximum_fusion, s32[8192]{0:T(1024)S(1)} %copy-done.2), kind=kCustom, calls=%fused_computation.2.clone | custom fusion | bytes 4227072 | tf_op jit(solution)/shard_map/jit(_take)/gather | solution.py:20
  476.5 29.2 %gather_fusion.3 = bf16[8192,128]{1,0:T(8,128)(2,1)} fusion(bf16[10368,128]{1,0:T(8,128)(2,1)S(1)} %pad_maximum_fusion, s32[8192]{0:T(1024)S(1)} %fusion.5), kind=kCustom, calls=%fused_computation.1.clone | custom fusion | bytes 4227072 | tf_op jit(solution)/shard_map/jit(_take)/gather | solution.py:20
  505.9 0.0 copy-start.39
  506.0 0.0 copy-start.41
  506.0 29.2 %gather_fusion.2 = bf16[8192,128]{1,0:T(8,128)(2,1)} fusion(bf16[10368,128]{1,0:T(8,128)(2,1)S(1)} %pad_maximum_fusion, s32[8192]{0:T(1024)S(1)} %fusion.4), kind=kCustom, calls=%fused_computation.clone | custom fusion | bytes 4227072 | tf_op jit(solution)/shard_map/jit(_take)/gather | solution.py:20
  535.5 56.1 %fusion.2 = bf16[8192,128]{1,0:T(8,128)(2,1)} fusion(f32[8192,128]{1,0:T(8,128)} %fusion.26, bf16[128,128]{1,0:T(8,128)(2,1)S(1)} %copy-done.39, f32[128]{0:T(128)S(1)} %copy-done.41, bf16[8192,128]{1,0:T(8,128)(2,1)} %gather_fusion.17, bf16[8192,128]{1,0:T(8,128)(2,1)} %gather_fusion.16, bf16[8192,128]{1,0:T(8,128)(2,1)} %gather_fusion.15, ...), kind=kOutput, calls=%fused_computation.21 | convolution fusion | flops 340787200 | bytes 40174080 | tf_op jit(solution)/shard_map/dot_general | solution.py:24
  (94 shorter events, 0.3 us)
Async XLA Ops:
  0.0 55.1 %copy-start = (bf16[128,128]{1,0:T(8,128)(2,1)S(1)}, bf16[128,128]{1,0:T(8,128)(2,1)}, u32[]{:S(2)}) copy-start(bf16[128,128]{1,0:T(8,128)(2,1)} %param.15) | copy-start | bytes 98308
  8.9 8.7 %copy-start.40 = (s32[1,8]{1,0:T(1,128)S(1)}, s32[1,8]{1,0:T(1,128)}, u32[]{:S(2)}) copy-start(s32[1,8]{1,0:T(1,128)} %param.14) | copy-start | bytes 100
  8.9 19.0 %copy-start.1 = (bf16[8192,128]{1,0:T(8,128)(2,1)S(1)}, bf16[8192,128]{1,0:T(8,128)(2,1)}, u32[]{:S(2)}) copy-start(bf16[8192,128]{1,0:T(8,128)(2,1)} %param.10) | copy-start | bytes 6291460
  10.0 42.0 %copy-start.7 = (s32[8192]{0:T(1024)S(1)}, s32[8192]{0:T(1024)}, u32[]{:S(2)}) copy-start(s32[8192]{0:T(1024)} %param.12) | copy-start | bytes 98308
  10.0 47.8 %all-to-all-start = ((bf16[16,128,128]{2,1,0:T(8,128)(2,1)}), bf16[16,128,128]{2,1,0:T(8,128)(2,1)S(1)}, u32[]{:S(2)}, u32[]{:S(2)}) async-start(bf16[16,128,128]{2,1,0:T(8,128)(2,1)} %broadcast_select_fusion), calls=%async_computation | async-start | bytes 1048576 | tf_op jit(solution)/shard_map/all_to_all | solution.py:11
  65.0 31.9 %copy-start.6 = (s32[8192]{0:T(1024)S(1)}, s32[8192]{0:T(1024)}, u32[]{:S(2)}) copy-start(s32[8192]{0:T(1024)} %fusion.18) | copy-start | bytes 98308
  272.1 29.2 %copy-start.3 = (s32[8192]{0:T(1024)S(1)}, s32[8192]{0:T(1024)}, u32[]{:S(2)}) copy-start(s32[8192]{0:T(1024)} %fusion.11) | copy-start | bytes 98308
  330.5 29.2 %copy-start.4 = (s32[8192]{0:T(1024)S(1)}, s32[8192]{0:T(1024)}, u32[]{:S(2)}) copy-start(s32[8192]{0:T(1024)} %fusion.9) | copy-start | bytes 98308
  388.9 29.2 %copy-start.5 = (s32[8192]{0:T(1024)S(1)}, s32[8192]{0:T(1024)}, u32[]{:S(2)}) copy-start(s32[8192]{0:T(1024)} %fusion.7) | copy-start | bytes 98308
  418.1 29.2 %copy-start.2 = (s32[8192]{0:T(1024)S(1)}, s32[8192]{0:T(1024)}, u32[]{:S(2)}) copy-start(s32[8192]{0:T(1024)} %fusion.6) | copy-start | bytes 98308
  505.7 29.5 %copy-start.8 = (f32[8192]{0:T(1024)S(1)}, f32[8192]{0:T(1024)}, u32[]{:S(2)}) copy-start(f32[8192]{0:T(1024)} %convert_element_type.74) | copy-start | bytes 98308
  505.7 29.5 %copy-start.9 = (pred[8192]{0:T(1024)(128)(4,1)S(1)}, pred[8192]{0:T(1024)(128)(4,1)}, u32[]{:S(2)}) copy-start(pred[8192]{0:T(1024)(128)(4,1)} %get-tuple-element.52) | copy-start | bytes 24580
  505.7 29.5 %copy-start.10 = (pred[8192]{0:T(1024)(128)(4,1)S(1)}, pred[8192]{0:T(1024)(128)(4,1)}, u32[]{:S(2)}) copy-start(pred[8192]{0:T(1024)(128)(4,1)} %get-tuple-element.53) | copy-start | bytes 24580
  505.7 29.5 %copy-start.11 = (pred[8192]{0:T(1024)(128)(4,1)S(1)}, pred[8192]{0:T(1024)(128)(4,1)}, u32[]{:S(2)}) copy-start(pred[8192]{0:T(1024)(128)(4,1)} %get-tuple-element.42) | copy-start | bytes 24580
  505.7 29.5 %copy-start.12 = (pred[8192]{0:T(1024)(128)(4,1)S(1)}, pred[8192]{0:T(1024)(128)(4,1)}, u32[]{:S(2)}) copy-start(pred[8192]{0:T(1024)(128)(4,1)} %get-tuple-element.43) | copy-start | bytes 24580
  505.7 29.5 %copy-start.13 = (pred[8192]{0:T(1024)(128)(4,1)S(1)}, pred[8192]{0:T(1024)(128)(4,1)}, u32[]{:S(2)}) copy-start(pred[8192]{0:T(1024)(128)(4,1)} %get-tuple-element.44) | copy-start | bytes 24580
  505.7 29.5 %copy-start.14 = (pred[8192]{0:T(1024)(128)(4,1)S(1)}, pred[8192]{0:T(1024)(128)(4,1)}, u32[]{:S(2)}) copy-start(pred[8192]{0:T(1024)(128)(4,1)} %get-tuple-element.45) | copy-start | bytes 24580
  505.7 29.5 %copy-start.15 = (pred[8192]{0:T(1024)(128)(4,1)S(1)}, pred[8192]{0:T(1024)(128)(4,1)}, u32[]{:S(2)}) copy-start(pred[8192]{0:T(1024)(128)(4,1)} %get-tuple-element.46) | copy-start | bytes 24580
  505.7 29.5 %copy-start.16 = (pred[8192]{0:T(1024)(128)(4,1)S(1)}, pred[8192]{0:T(1024)(128)(4,1)}, u32[]{:S(2)}) copy-start(pred[8192]{0:T(1024)(128)(4,1)} %get-tuple-element.47) | copy-start | bytes 24580
  505.7 29.5 %copy-start.17 = (pred[8192]{0:T(1024)(128)(4,1)S(1)}, pred[8192]{0:T(1024)(128)(4,1)}, u32[]{:S(2)}) copy-start(pred[8192]{0:T(1024)(128)(4,1)} %get-tuple-element.48) | copy-start | bytes 24580
  505.7 29.5 %copy-start.18 = (pred[8192]{0:T(1024)(128)(4,1)S(1)}, pred[8192]{0:T(1024)(128)(4,1)}, u32[]{:S(2)}) copy-start(pred[8192]{0:T(1024)(128)(4,1)} %get-tuple-element.49) | copy-start | bytes 24580
  505.7 29.5 %copy-start.19 = (pred[8192]{0:T(1024)(128)(4,1)S(1)}, pred[8192]{0:T(1024)(128)(4,1)}, u32[]{:S(2)}) copy-start(pred[8192]{0:T(1024)(128)(4,1)} %get-tuple-element.50) | copy-start | bytes 24580
  505.8 29.5 %copy-start.20 = (pred[8192]{0:T(1024)(128)(4,1)S(1)}, pred[8192]{0:T(1024)(128)(4,1)}, u32[]{:S(2)}) copy-start(pred[8192]{0:T(1024)(128)(4,1)} %get-tuple-element.51) | copy-start | bytes 24580
  505.8 29.5 %copy-start.21 = (pred[8192]{0:T(1024)(128)(4,1)S(1)}, pred[8192]{0:T(1024)(128)(4,1)}, u32[]{:S(2)}) copy-start(pred[8192]{0:T(1024)(128)(4,1)} %get-tuple-element.38) | copy-start | bytes 24580
  505.8 29.5 %copy-start.22 = (pred[8192]{0:T(1024)(128)(4,1)S(1)}, pred[8192]{0:T(1024)(128)(4,1)}, u32[]{:S(2)}) copy-start(pred[8192]{0:T(1024)(128)(4,1)} %get-tuple-element.39) | copy-start | bytes 24580
  505.8 29.5 %copy-start.23 = (pred[8192]{0:T(1024)(128)(4,1)S(1)}, pred[8192]{0:T(1024)(128)(4,1)}, u32[]{:S(2)}) copy-start(pred[8192]{0:T(1024)(128)(4,1)} %get-tuple-element.22) | copy-start | bytes 24580
  505.8 29.5 %copy-start.24 = (pred[8192]{0:T(1024)(128)(4,1)S(1)}, pred[8192]{0:T(1024)(128)(4,1)}, u32[]{:S(2)}) copy-start(pred[8192]{0:T(1024)(128)(4,1)} %get-tuple-element.23) | copy-start | bytes 24580
  505.8 29.5 %copy-start.25 = (pred[8192]{0:T(1024)(128)(4,1)S(1)}, pred[8192]{0:T(1024)(128)(4,1)}, u32[]{:S(2)}) copy-start(pred[8192]{0:T(1024)(128)(4,1)} %get-tuple-element.24) | copy-start | bytes 24580
  505.8 29.5 %copy-start.26 = (pred[8192]{0:T(1024)(128)(4,1)S(1)}, pred[8192]{0:T(1024)(128)(4,1)}, u32[]{:S(2)}) copy-start(pred[8192]{0:T(1024)(128)(4,1)} %get-tuple-element.25) | copy-start | bytes 24580
  505.8 29.5 %copy-start.27 = (pred[8192]{0:T(1024)(128)(4,1)S(1)}, pred[8192]{0:T(1024)(128)(4,1)}, u32[]{:S(2)}) copy-start(pred[8192]{0:T(1024)(128)(4,1)} %get-tuple-element.26) | copy-start | bytes 24580
  505.8 29.5 %copy-start.28 = (pred[8192]{0:T(1024)(128)(4,1)S(1)}, pred[8192]{0:T(1024)(128)(4,1)}, u32[]{:S(2)}) copy-start(pred[8192]{0:T(1024)(128)(4,1)} %get-tuple-element.27) | copy-start | bytes 24580
  505.8 29.5 %copy-start.29 = (pred[8192]{0:T(1024)(128)(4,1)S(1)}, pred[8192]{0:T(1024)(128)(4,1)}, u32[]{:S(2)}) copy-start(pred[8192]{0:T(1024)(128)(4,1)} %get-tuple-element.28) | copy-start | bytes 24580
  505.9 29.5 %copy-start.30 = (pred[8192]{0:T(1024)(128)(4,1)S(1)}, pred[8192]{0:T(1024)(128)(4,1)}, u32[]{:S(2)}) copy-start(pred[8192]{0:T(1024)(128)(4,1)} %get-tuple-element.29) | copy-start | bytes 24580
  505.9 29.5 %copy-start.31 = (pred[8192]{0:T(1024)(128)(4,1)S(1)}, pred[8192]{0:T(1024)(128)(4,1)}, u32[]{:S(2)}) copy-start(pred[8192]{0:T(1024)(128)(4,1)} %get-tuple-element.30) | copy-start | bytes 24580
  505.9 29.5 %copy-start.32 = (pred[8192]{0:T(1024)(128)(4,1)S(1)}, pred[8192]{0:T(1024)(128)(4,1)}, u32[]{:S(2)}) copy-start(pred[8192]{0:T(1024)(128)(4,1)} %get-tuple-element.31) | copy-start | bytes 24580
  505.9 29.5 %copy-start.33 = (pred[8192]{0:T(1024)(128)(4,1)S(1)}, pred[8192]{0:T(1024)(128)(4,1)}, u32[]{:S(2)}) copy-start(pred[8192]{0:T(1024)(128)(4,1)} %get-tuple-element.32) | copy-start | bytes 24580
  505.9 29.5 %copy-start.34 = (pred[8192]{0:T(1024)(128)(4,1)S(1)}, pred[8192]{0:T(1024)(128)(4,1)}, u32[]{:S(2)}) copy-start(pred[8192]{0:T(1024)(128)(4,1)} %get-tuple-element.33) | copy-start | bytes 24580
  505.9 29.5 %copy-start.35 = (pred[8192]{0:T(1024)(128)(4,1)S(1)}, pred[8192]{0:T(1024)(128)(4,1)}, u32[]{:S(2)}) copy-start(pred[8192]{0:T(1024)(128)(4,1)} %get-tuple-element.34) | copy-start | bytes 24580
  505.9 29.5 %copy-start.36 = (pred[8192]{0:T(1024)(128)(4,1)S(1)}, pred[8192]{0:T(1024)(128)(4,1)}, u32[]{:S(2)}) copy-start(pred[8192]{0:T(1024)(128)(4,1)} %get-tuple-element.35) | copy-start | bytes 24580
  505.9 29.5 %copy-start.37 = (pred[8192]{0:T(1024)(128)(4,1)S(1)}, pred[8192]{0:T(1024)(128)(4,1)}, u32[]{:S(2)}) copy-start(pred[8192]{0:T(1024)(128)(4,1)} %get-tuple-element.36) | copy-start | bytes 24580
  505.9 29.5 %copy-start.38 = (pred[8192]{0:T(1024)(128)(4,1)S(1)}, pred[8192]{0:T(1024)(128)(4,1)}, u32[]{:S(2)}) copy-start(pred[8192]{0:T(1024)(128)(4,1)} %get-tuple-element.37) | copy-start | bytes 24580
  505.9 29.5 %copy-start.39 = (bf16[128,128]{1,0:T(8,128)(2,1)S(1)}, bf16[128,128]{1,0:T(8,128)(2,1)}, u32[]{:S(2)}) copy-start(bf16[128,128]{1,0:T(8,128)(2,1)} %param.16) | copy-start | bytes 98308
  506.0 29.5 %copy-start.41 = (f32[128]{0:T(128)S(1)}, f32[128]{0:T(128)}, u32[]{:S(2)}) copy-start(f32[128]{0:T(128)} %param.17) | copy-start | bytes 1540
where the time goes:
time: 593 us; the launch traced here: 592 us
  local copies, waits for them, and re-layouts  481 us (81%)
  matrix products  58.8 us (10%)
  blocking collectives  22.9 us (4%)
  other arithmetic  20.4 us (3%)
  starting transfers between devices  7.52 us (1%)
    gather x16, local copies, waits for them, and re-layouts, local(): picked = jnp.take(table, neighbors[:, slot], axis=0).astype(jnp.float32)  470 us
    dot_general x1, matrix products, local(): jnp.dot(aggregate, w_neigh, preferred_element_type=jnp.float32)  56.1 us
    all_gather x1, blocking collectives, local(): hubs = lax.all_gather(mine, 'node', axis=0, tiled=True)  22.9 us
  transfers between devices with their start and end apart: 1, of which 0 were waited for; matrix products, arithmetic and copies ran while one was open for 3% of the time, Pallas kernels for 0%

commit v1 on v0

v1 whole, which is shorter than its diff:
```python
import functools

import jax
import jax.numpy as jnp
from jax import lax
from jax.experimental import pallas as pl
from jax.experimental.pallas import tpu as pltpu
from jax.sharding import PartitionSpec as P

F8 = jnp.float8_e4m3fn
BF16 = jnp.bfloat16
F32 = jnp.float32
LO = 256
VMEM_BYTES = 56 * 2**20


def outgoing_kernel(send_ref, hub_ref, feat_ref, out_ref, wide, picked, *, peers, rows, hubs, block):
    nodes = feat_ref.shape[0]

    @pl.loop(0, nodes // 256)
    def _(step):
        at = pl.ds(pl.multiple_of(step * 256, 256), 256)
        wide[at, :] = feat_ref[at, :].astype(F32)

    picked[...] = jnp.zeros_like(picked)
    for j in range(hubs):
        picked[rows + j : rows + j + 1, :] = wide[pl.ds(hub_ref[j], 1), :]

    @pl.loop(0, peers)
    def _(peer):
        for c in range(rows):
            picked[c : c + 1, :] = wide[pl.ds(send_ref[peer * rows + c], 1), :]
        at = pl.ds(pl.multiple_of(peer * block, 16), block)
        out_ref[at, :] = picked[...].astype(BF16)


def split(values):
    scaled = values.astype(F32) * 64.0
    high = scaled.astype(F8)
    low = ((scaled - high.astype(F32)) * 16.0).astype(F8)
    return high, low


def count_tile(row, group, highs):
    lanes = row.shape[1]
    per = lanes // group
    high = lax.shift_right_arithmetic(row, 8)
    low = row & (LO - 1)
    lane_node = lax.broadcasted_iota(jnp.int32, (2 * group, lanes), 1) // per
    sub = lax.broadcasted_iota(jnp.int32, (2 * group, lanes), 0)
    mine = jnp.where(lane_node == sub % group, jnp.broadcast_to(high, (2 * group, lanes)) - sub // group, -100).astype(jnp.int8)
    one = jnp.ones((2 * group, lanes), F8)
    zero = jnp.zeros((2 * group, lanes), F8)
    left = jnp.concatenate([jnp.where(mine == jnp.int8(2 * j), one, zero) for j in range(highs // 2)], axis=0)
    lows = jnp.broadcast_to(low - 128, (32, lanes)).astype(jnp.int8)
    sub = lax.broadcasted_iota(jnp.int32, (32, lanes), 0)
    one = jnp.ones((32, lanes), F8)
    zero = jnp.zeros((32, lanes), F8)
    right = jnp.concatenate(
        [jnp.where(lows == (sub + (32 * j - 128)).astype(jnp.int8), one, zero) for j in range(LO // 32)], axis=0
    )
    counts = lax.dot_general(left, right, (((1,), (1,)), ((), ())), preferred_element_type=F32)
    return counts.reshape(highs, group, LO)


def layer_kernel(
    index_ref, degree_ref, feat_ref, halo_ref, self_ref, neigh_ref, bias_ref, out_ref, table, counts, hub_rows, *, tile, group, peers, rows, hubs, block, highs, unroll
):
    nodes, width = feat_ref.shape
    step = pl.program_id(0)

    def put(at, size, values):
        high, low = split(values)
        table[pl.ds(at, size), :width] = high
        table[pl.ds(at, size), width:] = low

    @pl.when(step == 0)
    def _():
        @pl.loop(0, nodes // 256)
        def _(i):
            at = pl.multiple_of(i * 256, 256)
            put(at, 256, feat_ref[pl.ds(at, 256), :])

        hub_rows[...] = jnp.zeros_like(hub_rows)

        @pl.loop(0, peers)
        def _(i):
            at = pl.multiple_of(i * block, 16)
            put(pl.multiple_of(nodes + i * rows, 32), rows, halo_ref[pl.ds(at, rows), :])
            tail = halo_ref[pl.ds(at + rows, block - rows), :].astype(F32)
            hub_rows[pl.ds(pl.multiple_of(i * hubs, 8), hubs), :] = tail[:hubs, :]

        put(nodes + peers * rows, hub_rows.shape[0], hub_rows[...])

    def pair(i, carry):
        both = [count_tile(index_ref[pl.ds(2 * i + j, 1), :], group, highs) for j in range(2)]
        both = jnp.concatenate(both, axis=1).astype(F8)
        at = pl.ds(pl.multiple_of(i * 2 * group, 2 * group), 2 * group)
        for h in range(highs):
            counts[at, h * LO : (h + 1) * LO] = both[h]
        return carry

    lax.fori_loop(0, tile // (2 * group), pair, 0, unroll=unroll)
    total = jnp.dot(counts[...], table[...], preferred_element_type=F32)
    total = total[:, :width] * (1.0 / 64.0) + total[:, width:] * (1.0 / 1024.0)
    eye = lax.broadcasted_iota(jnp.int32, (128, 128), 0) == lax.broadcasted_iota(jnp.int32, (128, 128), 1)
    ones = jnp.ones((128, width), BF16)
    spread = []
    for j in range(tile // 128):
        line = degree_ref[pl.ds(step * (tile // 128) + j, 1), :].astype(F32)
        spread.append(jnp.dot(jnp.where(eye, line, 0.0).astype(BF16), ones, preferred_element_type=F32))
    aggregate = (total / jnp.concatenate(spread, axis=0)).astype(BF16)
    own = feat_ref[pl.ds(pl.multiple_of(step * tile, tile), tile), :]
    mixed = jnp.dot(own, self_ref[...], preferred_element_type=F32)
    mixed = mixed + jnp.dot(aggregate, neigh_ref[...], preferred_element_type=F32) + bias_ref[...]
    out_ref[...] = jnp.maximum(mixed, 0.0).astype(BF16)


def local(features, neighbors, degree, send_list, hub_rows, w_self, w_neigh, bias):
    nodes, width = features.shape
    fanout = neighbors.shape[1]
    _, peers, rows = send_list.shape
    hubs = hub_rows.shape[1]
    block = -(-(rows + hubs) // 16) * 16
    group = 256 // fanout
    highs = -(-(nodes + peers * (rows + hubs)) // (2 * LO)) * 2
    hub_space = highs * LO - nodes - peers * rows
    tile = 512
    smem = pl.BlockSpec(memory_space=pltpu.SMEM)
    vmem = pl.BlockSpec(memory_space=pltpu.VMEM)

    outgoing = pl.pallas_call(
        functools.partial(outgoing_kernel, peers=peers, rows=rows, hubs=hubs, block=block),
        in_specs=[smem, smem, vmem],
        out_specs=vmem,
        out_shape=jax.ShapeDtypeStruct((peers * block, width), BF16),
        scratch_shapes=[pltpu.VMEM((nodes, width), F32), pltpu.VMEM((block, width), F32)],
        compiler_params=pltpu.CompilerParams(vmem_limit_bytes=VMEM_BYTES),
        name="outgoing_rows",
    )(send_list.reshape(-1), hub_rows.reshape(-1), features)
    halo = lax.all_to_all(outgoing.reshape(peers, block, width), "node", split_axis=0, concat_axis=0, tiled=True)
    halo = halo.reshape(peers * block, width)

    slots = lax.broadcasted_iota(jnp.int32, (nodes, fanout), 1)
    index = jnp.where(slots < degree[:, None], neighbors, -1).reshape(nodes // group, group * fanout)
    kernel = functools.partial(
        layer_kernel, tile=tile, group=group, peers=peers, rows=rows, hubs=hubs, block=block, highs=highs, unroll=8
    )
    whole = lambda *shape: pl.BlockSpec(shape, lambda i: (0,) * len(shape))
    return pl.pallas_call(
        kernel,
        grid=(nodes // tile,),
        in_specs=[
            pl.BlockSpec((tile // group, group * fanout), lambda i: (i, 0)),
            whole(nodes // 128, 128),
            whole(nodes, width),
            whole(peers * block, width),
            whole(width, width),
            whole(width, width),
            whole(1, width),
        ],
        out_specs=pl.BlockSpec((tile, width), lambda i: (i, 0)),
        out_shape=jax.ShapeDtypeStruct((nodes, width), BF16),
        scratch_shapes=[
            pltpu.VMEM((highs * LO, 2 * width), F8),
            pltpu.VMEM((tile, highs * LO), F8),
            pltpu.VMEM((hub_space, width), F32),
        ],
        compiler_params=pltpu.CompilerParams(vmem_limit_bytes=VMEM_BYTES),
        name="sage_layer",
    )(index, degree.reshape(nodes // 128, 128), features, halo, w_self, w_neigh, bias.reshape(1, width))


def solution(mesh):
    in_specs = (
        P(("groups", "node"), None),
        P(("groups", "node"), None),
        P(("groups", "node")),
        P(("groups", "node"), None, None),
        P(("groups", "node"), None),
        P(),
        P(),
        P(),
    )
    out_specs = P(("groups", "node"), None)
    return jax.shard_map(local, mesh=mesh, in_specs=in_specs, out_specs=out_specs, check_vma=False)
```

time: 593 us -> 90.2 us (0.15)
  local copies, waits for them, and re-layouts: 481 us -> 7.65 us
  Pallas kernels: 0 us -> 66.1 us
  matrix products: 58.8 us -> 0 us
  blocking collectives: 22.9 us -> 0 us
  other arithmetic: 20.4 us -> 0.05 us
  waiting for transfers between devices: 0.01 us -> 8.66 us
    gather x18 -> x0, local copies, waits for them, and re-layouts: 478 us -> none  [the longest x16 470 us: local(): picked = jnp.take(table, neighbors[:, slot], axis=0).astype(jnp.float32)]
    pallas_call x0 -> x2, Pallas kernels: none -> 66.1 us  [the longest x1 61.3 us: local(): pl.pallas_call(kernel, grid=(nodes // tile,), in_specs=[pl.BlockSpec((til...]
    dot_general x2 -> x0, matrix products: 58.8 us -> none  [the longest x1 56.1 us: local(): jnp.dot(aggregate, w_neigh, preferred_element_type=jnp.float32)]
    all_gather x1 -> x0, blocking collectives: 22.9 us -> none  [local(): hubs = lax.all_gather(mine, 'node', axis=0, tiled=True)]
    all_to_all x1, waiting for transfers between devices: 0.01 us -> 8.66 us  [local(): lax.all_to_all(outgoing.reshape(peers, block, width), 'node', split_axis=...]
    concatenate x1 -> x0, other arithmetic: 7.19 us -> none  [local(): table = jnp.concatenate([features, halo, hubs], axis=0)]
  transfers between devices with their start and end apart: 1 -> 1, of which waited for: 0 -> 1; matrix products, arithmetic and copies ran while one was open for 3% -> 8% of each run, Pallas kernels for 0% -> 0%
where the time goes in v1:
time: 90.2 us; the launch traced here: 89.9 us
  Pallas kernels  66.1 us (73%)
  waiting for transfers between devices  8.66 us (10%)
  local copies, waits for them, and re-layouts  7.65 us (8%)
  starting transfers between devices  7.39 us (8%)
    pallas_call x1, Pallas kernels, local(): pl.pallas_call(kernel, grid=(nodes // tile,), in_specs=[pl.BlockSpec((til...  61.3 us
    all_to_all x1, waiting for transfers between devices, local(): lax.all_to_all(outgoing.reshape(peers, block, width), 'node', split_axis=...  8.66 us
    all_to_all x1, starting transfers between devices, local(): lax.all_to_all(outgoing.reshape(peers, block, width), 'node', split_axis=...  7.39 us
    pallas_call x1, Pallas kernels, local(): pl.pallas_call(functools.partial(outgoing_kernel, peers=peers, rows=rows,...  4.82 us
    reshape x1, local copies, waits for them, and re-layouts, local(): jnp.where(slots < degree[:, None], neighbors, -1)  4.2 us
    select_n x1, local copies, waits for them, and re-layouts, local(): jnp.where(slots < degree[:, None], neighbors, -1)  2.61 us
  transfers between devices with their start and end apart: 1, of which 1 were waited for; matrix products, arithmetic and copies ran while one was open for 8% of the time, Pallas kernels for 0%

profile of v1, /device:TPU:0, one launch (start us, length us, event | category | flops | bytes accessed | tf_op | source)
XLA Modules:
  0.0 89.9 jit_solution(9967929943824155355)
XLA Ops:
  0.0 0.0 copy-start.2
  0.0 0.0 copy-start.1
  0.0 4.8 %outgoing_rows.1 = bf16[2304,128]{1,0:T(8,128)(2,1)} custom-call(s32[2048]{0:T(1024)} %bitcast.9, s32[8]{0:T(128)} %bitcast.10, bf16[8192,128]{1,0:T(8,128)(2,1)} %feat_ref.3), custom_call_target="tpu_custom_call" | custom-call | tf_op jit(solution)/shard_map/outgoing_rows/pallas_call | solution.py:132
  4.8 7.4 %all-to-all-start = ((bf16[16,144,128]{2,1,0:T(8,128)(2,1)}), bf16[16,144,128]{2,1,0:T(8,128)(2,1)S(1)}, u32[]{:S(2)}, u32[]{:S(2)}) async-start(bf16[16,144,128]{2,1,0:T(8,128)(2,1)} %bitcast.7), calls=%async_computation | async-start | bytes 1179648 | tf_op jit(solution)/shard_map/all_to_all | solution.py:141
  12.2 0.0 copy-done.2
  12.2 0.0 copy-done.1
  12.3 2.6 %copy.10 = s32[8192,16]{1,0:T(8,128)} copy(s32[8192,16]{0,1:T(8,128)S(1)} %fusion) | data formatting | bytes 1048576 | tf_op jit(solution)/shard_map/jit(_where)/select_n | solution.py:145
  14.9 4.2 %reshape.22.index_ref = s32[512,256]{1,0:T(8,128)} reshape(s32[8192,16]{1,0:T(8,128)} %copy.10) | data formatting | bytes 1048576 | tf_op jit(solution)/shard_map/reshape | solution.py:145
  19.1 8.7 %all-to-all-done = bf16[16,144,128]{2,1,0:T(8,128)(2,1)S(1)} async-done(((bf16[16,144,128]{2,1,0:T(8,128)(2,1)}), bf16[16,144,128]{2,1,0:T(8,128)(2,1)S(1)}, u32[]{:S(2)}, u32[]{:S(2)}) %all-to-all-start) | async-done | bytes 589856 | tf_op jit(solution)/shard_map/all_to_all | solution.py:141
  27.8 0.0 copy-start
  27.8 0.8 copy-done
  28.6 61.3 %sage_layer.1 = bf16[8192,128]{1,0:T(8,128)(2,1)} custom-call(s32[512,256]{1,0:T(8,128)} %reshape.22.index_ref, s32[64,128]{1,0:T(8,128)} %bitcast.8, bf16[8192,128]{1,0:T(8,128)(2,1)} %feat_ref.3, bf16[2304,128]{1,0:T(8,128)(2,1)} %bitcast.6, bf16[128,128]{1,0:T(8,128)(2,1)} %self_ref.1, bf16[128,128]{1,0:T(8,128)(2,1)} %neigh_ref.1, f32[1,128]{1,0:T(1,128)} %bitcast.11), custom_call_target="tpu_custom_call" | custom-call | tf_op jit(solution)/shard_map/sage_layer/pallas_call | solution.py:150
  (1 shorter events, 0.0 us)
Async XLA Ops:
  0.0 12.2 %copy-start.2 = (s32[8192]{0:T(1024)S(1)}, s32[8192]{0:T(1024)}, u32[]{:S(2)}) copy-start(s32[8192]{0:T(1024)} %param.10) | copy-start | bytes 98308
  0.0 12.2 %copy-start.1 = (s32[8192,16]{0,1:T(8,128)S(1)}, s32[8192,16]{0,1:T(8,128)}, u32[]{:S(2)}) copy-start(s32[8192,16]{0,1:T(8,128)} %param.9) | copy-start | bytes 1572868
  4.8 22.9 %all-to-all-start = ((bf16[16,144,128]{2,1,0:T(8,128)(2,1)}), bf16[16,144,128]{2,1,0:T(8,128)(2,1)S(1)}, u32[]{:S(2)}, u32[]{:S(2)}) async-start(bf16[16,144,128]{2,1,0:T(8,128)(2,1)} %bitcast.7), calls=%async_computation | async-start | bytes 1179648 | tf_op jit(solution)/shard_map/all_to_all | solution.py:141
  27.8 0.8 copy-start

commit v2 on v1

v2 whole, which is shorter than its diff:
```python
import functools

import jax
import jax.numpy as jnp
from jax import lax
from jax.experimental import pallas as pl
from jax.experimental.pallas import tpu as pltpu
from jax.sharding import PartitionSpec as P

F8 = jnp.float8_e4m3fn
BF16 = jnp.bfloat16
F32 = jnp.float32
LO = 256
VMEM_BYTES = 56 * 2**20


def outgoing_kernel(send_ref, hub_ref, feat_ref, out_ref, wide, picked, *, peers, rows, hubs):
    nodes = feat_ref.shape[0]
    block = rows + hubs

    @pl.loop(0, nodes // 256)
    def _(step):
        at = pl.ds(pl.multiple_of(step * 256, 256), 256)
        wide[at, :] = feat_ref[at, :].astype(F32)

    mine = jnp.concatenate([wide[pl.ds(hub_ref[j], 1), :] for j in range(hubs)], axis=0)

    @pl.loop(0, peers)
    def _(peer):
        to = picked.at[pl.ds(pl.multiple_of(peer * block, 8), block)]
        for c in range(rows):
            to[c : c + 1, :] = wide[pl.ds(send_ref[peer * rows + c], 1), :]
        to[rows:, :] = mine

    out_ref[...] = picked[...].astype(BF16)


def split(values):
    scaled = values.astype(F32) * 64.0
    high = scaled.astype(F8)
    low = ((scaled - high.astype(F32)) * 16.0).astype(F8)
    return jnp.concatenate([high, low], axis=1)


def joined(total):
    width = total.shape[1] // 2
    return total[:, :width] * (1.0 / 64.0) + total[:, width:] * (1.0 / 1024.0)


def count_group(row, group, first, last):
    lanes = row.shape[1]
    per = lanes // group
    high = lax.shift_right_arithmetic(row, 8)
    low = row & (LO - 1)
    shape = (2 * group, lanes)
    lane_node = lax.broadcasted_iota(jnp.int32, shape, 1) // per
    sub = lax.broadcasted_iota(jnp.int32, shape, 0)
    mine = jnp.where(lane_node == sub % group, jnp.broadcast_to(high, shape) - sub // group, -100).astype(jnp.int8)
    one = jnp.ones(shape, F8)
    zero = jnp.zeros(shape, F8)
    left = jnp.concatenate([jnp.where(mine == jnp.int8(j), one, zero) for j in range(first, last, 2)], axis=0)
    lows = jnp.broadcast_to(low - 128, shape).astype(jnp.int8)
    right = jnp.concatenate(
        [jnp.where(lows == (sub + (j - 128)).astype(jnp.int8), one, zero) for j in range(0, LO, 2 * group)], axis=0
    )
    counts = lax.dot_general(left, right, (((1,), (1,)), ((), ())), preferred_element_type=F32)
    return counts.reshape(last - first, group, LO)


def fill_counts(counts, index_ref, base, tile, group, first, last, unroll):
    def pair(i, carry):
        both = [count_group(index_ref[pl.ds(base + 2 * i + j, 1), :], group, first, last) for j in range(2)]
        both = jnp.concatenate(both, axis=1).astype(F8)
        at = pl.ds(pl.multiple_of(i * 2 * group, 2 * group), 2 * group)
        for h in range(last - first):
            counts[at, h * LO : (h + 1) * LO] = both[h]
        return carry

    lax.fori_loop(0, tile // (2 * group), pair, 0, unroll=unroll)


def own_kernel(slot_ref, degree_ref, feat_ref, index_ref, table_ref, part_ref, counts, *, tile, early, group, fanout, own):
    nodes, width = feat_ref.shape
    lanes = group * fanout
    half = nodes // 128 * 8

    pick = lax.broadcasted_iota(jnp.int32, (fanout, lanes), 0) == lax.broadcasted_iota(jnp.int32, (fanout, lanes), 1) % fanout
    pick = jnp.where(pick, 1.0, 0.0).astype(BF16)
    slot = lax.broadcasted_iota(jnp.int32, (fanout, 128), 0)
    sub = lax.broadcasted_iota(jnp.int32, (128, lanes), 0)
    keep = sub % group == lax.broadcasted_iota(jnp.int32, (128, lanes), 1) // fanout

    def relay(i, carry):
        at = pl.multiple_of(i * 8, 8)
        lines = jnp.concatenate([slot_ref[pl.ds(at + half * j, 8), :] for j in range(fanout // 8)], axis=0)
        lines = jnp.where(slot < degree_ref[pl.ds(i, 1), :], lines, -1)
        high = lax.shift_right_arithmetic(lines, 8).astype(F32).astype(BF16)
        low = (lines & 255).astype(F32).astype(BF16)
        turned = [
            lax.dot_general(part, pick, (((0,), (0,)), ((), ())), preferred_element_type=F32) for part in (high, low)
        ]
        turned = jnp.where(keep, turned[0] * 256.0 + turned[1], 0.0)
        rows = [jnp.sum(turned[g * group : (g + 1) * group], axis=0, keepdims=True) for g in range(128 // group)]
        index_ref[pl.ds(pl.multiple_of(i * (128 // group), 128 // group), 128 // group), :] = jnp.concatenate(rows, axis=0).astype(
            jnp.int32
        )
        return carry

    lax.fori_loop(0, nodes // 128, relay, 0, unroll=2)

    @pl.loop(0, nodes // 256)
    def _(i):
        at = pl.ds(pl.multiple_of(i * 256, 256), 256)
        table_ref[at, :] = split(feat_ref[at, :])

    @pl.loop(0, early // tile)
    def _(t):
        fill_counts(counts, index_ref, t * (tile // group), tile, group, 0, own, 8)
        total = jnp.dot(counts[...], table_ref[...], preferred_element_type=F32)
        part_ref[pl.ds(pl.multiple_of(t * tile, tile), tile), :] = joined(total)


def layer_kernel(
    index_ref, degree_ref, part_ref, feat_ref, halo_ref, table_ref, self_ref, neigh_ref, bias_ref, out_ref,
    table, counts, wide, hub_rows, sem, *, tile, early, group, peers, rows, hubs, own, highs
):
    nodes, width = table_ref.shape[0], feat_ref.shape[1]
    step = pl.program_id(0)
    block = rows + hubs

    @pl.when(step == 0)
    def _():
        copy = pltpu.make_async_copy(table_ref, table.at[pl.ds(0, nodes)], sem)
        copy.start()
        wide[...] = halo_ref[...].astype(F32)
        hub_rows[...] = jnp.zeros_like(hub_rows)

        @pl.loop(0, peers)
        def _(i):
            at = pl.multiple_of(i * block, 8)
            table[pl.ds(pl.multiple_of(nodes + i * rows, 32), rows), :] = split(wide[pl.ds(at, rows), :])
            hub_rows[pl.ds(pl.multiple_of(i * hubs, 8), hubs), :] = wide[pl.ds(at + rows, hubs), :]

        table[nodes + peers * rows :, :] = split(hub_rows[...])
        copy.wait()

    def finish(total):
        eye = lax.broadcasted_iota(jnp.int32, (128, 128), 0) == lax.broadcasted_iota(jnp.int32, (128, 128), 1)
        ones = jnp.ones((128, width), BF16)
        spread = []
        for j in range(tile // 128):
            line = degree_ref[pl.ds(step * (tile // 128) + j, 1), :].astype(F32)
            spread.append(jnp.dot(jnp.where(eye, line, 0.0).astype(BF16), ones, preferred_element_type=F32))
        aggregate = (total / jnp.concatenate(spread, axis=0)).astype(BF16)
        mixed = jnp.dot(feat_ref[...], self_ref[...], preferred_element_type=F32)
        mixed = mixed + jnp.dot(aggregate, neigh_ref[...], preferred_element_type=F32) + bias_ref[...]
        out_ref[...] = jnp.maximum(mixed, 0.0).astype(BF16)

    @pl.when(step < early // tile)
    def _():
        fill_counts(counts, index_ref, 0, tile, group, own, highs, 8)
        total = jnp.dot(counts[:, : (highs - own) * LO], table[own * LO :, :], preferred_element_type=F32)
        finish(joined(total) + part_ref[...])

    @pl.when(step >= early // tile)
    def _():
        fill_counts(counts, index_ref, 0, tile, group, 0, highs, 8)
        finish(joined(jnp.dot(counts[...], table[...], preferred_element_type=F32)))


def local(features, neighbors, degree, send_list, hub_rows, w_self, w_neigh, bias):
    nodes, width = features.shape
    fanout = neighbors.shape[1]
    _, peers, rows = send_list.shape
    hubs = hub_rows.shape[1]
    block = rows + hubs
    group = 256 // fanout
    own = nodes // LO
    highs = -(-(nodes + peers * block) // (2 * LO)) * 2
    hub_space = highs * LO - nodes - peers * rows
    tile = 512
    early = 2048
    smem = pl.BlockSpec(memory_space=pltpu.SMEM)
    vmem = pl.BlockSpec(memory_space=pltpu.VMEM)
    params = pltpu.CompilerParams(vmem_limit_bytes=VMEM_BYTES)

    outgoing = pl.pallas_call(
        functools.partial(outgoing_kernel, peers=peers, rows=rows, hubs=hubs),
        in_specs=[smem, smem, vmem],
        out_specs=vmem,
        out_shape=jax.ShapeDtypeStruct((peers * block, width), BF16),
        scratch_shapes=[pltpu.VMEM((nodes, width), F32), pltpu.VMEM((peers * block, width), F32)],
        compiler_params=params,
        name="outgoing_rows",
    )(send_list.reshape(-1), hub_rows.reshape(-1), features)
    halo = lax.all_to_all(outgoing.reshape(peers, block, width), "node", split_axis=0, concat_axis=0, tiled=True)
    halo = halo.reshape(peers * block, width)

    lines = neighbors.T.reshape(fanout // 8, 8, nodes // 128, 128).transpose(0, 2, 1, 3).reshape(-1, 128)
    counts_of = degree.reshape(nodes // 128, 128)
    index, table, part = pl.pallas_call(
        functools.partial(own_kernel, tile=tile, early=early, group=group, fanout=fanout, own=own),
        in_specs=[vmem, vmem, vmem],
        out_specs=[vmem, vmem, vmem],
        out_shape=[
            jax.ShapeDtypeStruct((nodes // group, group * fanout), jnp.int32),
            jax.ShapeDtypeStruct((nodes, 2 * width), F8),
            jax.ShapeDtypeStruct((early, width), F32),
        ],
        scratch_shapes=[pltpu.VMEM((tile, own * LO), F8)],
        compiler_params=params,
        cost_estimate=pl.CostEstimate(flops=30_000_000_000, bytes_accessed=6_000_000, transcendentals=0),
        name="own_part",
    )(lines, counts_of, features)

    whole = lambda *shape: pl.BlockSpec(shape, lambda i: (0,) * len(shape))
    last_early = early // tile - 1
    return pl.pallas_call(
        functools.partial(
            layer_kernel, tile=tile, early=early, group=group, peers=peers, rows=rows, hubs=hubs, own=own, highs=highs
        ),
        grid=(nodes // tile,),
        in_specs=[
            pl.BlockSpec((tile // group, group * fanout), lambda i: (i, 0)),
            whole(nodes // 128, 128),
            pl.BlockSpec((tile, width), lambda i: (jnp.minimum(i, last_early), 0)),
            pl.BlockSpec((tile, width), lambda i: (i, 0)),
            whole(peers * block, width),
            pl.BlockSpec(memory_space=pl.ANY),
            whole(width, width),
            whole(width, width),
            whole(1, width),
        ],
        out_specs=pl.BlockSpec((tile, width), lambda i: (i, 0)),
        out_shape=jax.ShapeDtypeStruct((nodes, width), BF16),
        scratch_shapes=[
            pltpu.VMEM((highs * LO, 2 * width), F8),
            pltpu.VMEM((tile, highs * LO), F8),
            pltpu.VMEM((peers * block, width), F32),
            pltpu.VMEM((hub_space, width), F32),
            pltpu.SemaphoreType.DMA,
        ],
        compiler_params=params,
        name="sage_layer",
    )(index, counts_of, part, features, halo, table, w_self, w_neigh, bias.reshape(1, width))


def solution(mesh):
    in_specs = (
        P(("groups", "node"), None),
        P(("groups", "node"), None),
        P(("groups", "node")),
        P(("groups", "node"), None, None),
        P(("groups", "node"), None),
        P(),
        P(),
        P(),
    )
    out_specs = P(("groups", "node"), None)
    return jax.shard_map(local, mesh=mesh, in_specs=in_specs, out_specs=out_specs, check_vma=False)
```

time: 90.2 us -> 89.9 us (level)
  Pallas kernels: 66.1 us -> 81.4 us
  waiting for transfers between devices: 8.66 us -> 0.01 us
  local copies, waits for them, and re-layouts: 7.65 us -> 0.81 us
    pallas_call x1 -> x2, Pallas kernels: 61.3 us -> 76.8 us  [the longest x1 53.6 us: local(): pl.pallas_call(functools.partial(layer_kernel, tile=tile, early=early, gr...]
    all_to_all x1, waiting for transfers between devices: 8.66 us -> 0.01 us  [local(): lax.all_to_all(outgoing.reshape(peers, block, width), 'node', split_axis=...]
    reshape x1 -> x0, local copies, waits for them, and re-layouts: 4.2 us -> none  [local(): jnp.where(slots < degree[:, None], neighbors, -1)]
    select_n x1 -> x0, local copies, waits for them, and re-layouts: 2.61 us -> none  [local(): jnp.where(slots < degree[:, None], neighbors, -1)]
  transfers between devices with their start and end apart: 1 -> 1, of which waited for: 1 -> 0; matrix products, arithmetic and copies ran while one was open for 8% -> 0% of each run, Pallas kernels for 0% -> 26%
where the time goes in v2:
time: 89.9 us; the launch traced here: 89.6 us
  Pallas kernels  81.4 us (91%)
  starting transfers between devices  7.39 us (8%)
    pallas_call x1, Pallas kernels, local(): pl.pallas_call(functools.partial(layer_kernel, tile=tile, early=early, gr...  53.6 us
    pallas_call x1, Pallas kernels, local(): pl.pallas_call(functools.partial(own_kernel, tile=tile, early=early, grou...  23.2 us
    all_to_all x1, starting transfers between devices, local(): lax.all_to_all(outgoing.reshape(peers, block, width), 'node', split_axis=...  7.39 us
    pallas_call x1, Pallas kernels, local(): pl.pallas_call(functools.partial(outgoing_kernel, peers=peers, rows=rows,...  4.57 us
  transfers between devices with their start and end apart: 1, of which 0 were waited for; matrix products, arithmetic and copies ran while one was open for 0% of the time, Pallas kernels for 26%

profile of v2, /device:TPU:0, one launch (start us, length us, event | category | flops | bytes accessed | tf_op | source)
XLA Modules:
  0.0 89.6 jit_solution(7852797910466540188)
XLA Ops:
  0.0 4.6 %outgoing_rows.1 = bf16[2176,128]{1,0:T(8,128)(2,1)} custom-call(s32[2048]{0:T(1024)} %bitcast.17, s32[8]{0:T(128)} %bitcast.18, bf16[8192,128]{1,0:T(8,128)(2,1)} %feat_ref.5), custom_call_target="tpu_custom_call" | custom-call | tf_op jit(solution)/shard_map/outgoing_rows/pallas_call | solution.py:187
  4.6 7.4 %all-to-all-start = ((bf16[16,136,128]{2,1,0:T(8,128)(2,1)}), bf16[16,136,128]{2,1,0:T(8,128)(2,1)S(1)}, u32[]{:S(2)}, u32[]{:S(2)}) async-start(bf16[16,136,128]{2,1,0:T(8,128)(2,1)} %bitcast.14), calls=%async_computation | async-start | bytes 1114112 | tf_op jit(solution)/shard_map/all_to_all | solution.py:196
  12.0 23.2 %own_part.1 = (s32[512,256]{1,0:T(8,128)}, f8e4m3fn[8192,256]{1,0:T(32,128)(4,1)}, f32[2048,128]{1,0:T(8,128)}) custom-call(s32[1024,128]{1,0:T(8,128)} %bitcast.20, s32[64,128]{1,0:T(8,128)} %bitcast.15, bf16[8192,128]{1,0:T(8,128)(2,1)} %feat_ref.5), custom_call_target="tpu_custom_call" | custom-call | flops 30000001024 | bytes 6000000 | tf_op jit(solution)/shard_map/own_part/pallas_call | solution.py:201
  35.2 0.0 all-to-all-done
  35.2 0.0 copy-start
  35.2 0.8 copy-done
  36.0 53.6 %sage_layer.1 = bf16[8192,128]{1,0:T(8,128)(2,1)} custom-call(s32[512,256]{1,0:T(8,128)} %get-tuple-element.8.index_ref, s32[64,128]{1,0:T(8,128)} %bitcast.16, f32[2048,128]{1,0:T(8,128)} %get-tuple-element.9.part_ref, bf16[8192,128]{1,0:T(8,128)(2,1)} %feat_ref.5, bf16[2176,128]{1,0:T(8,128)(2,1)} %bitcast.13, ...), custom_call_target="tpu_custom_call" | custom-call | tf_op jit(solution)/shard_map/sage_layer/pallas_call | solution.py:218
Async XLA Ops:
  4.6 30.6 %all-to-all-start = ((bf16[16,136,128]{2,1,0:T(8,128)(2,1)}), bf16[16,136,128]{2,1,0:T(8,128)(2,1)S(1)}, u32[]{:S(2)}, u32[]{:S(2)}) async-start(bf16[16,136,128]{2,1,0:T(8,128)(2,1)} %bitcast.14), calls=%async_computation | async-start | bytes 1114112 | tf_op jit(solution)/shard_map/all_to_all | solution.py:196
  35.2 0.8 copy-start

commit v3 on v2

--- a/solution.py
+++ b/solution.py
@@ -12,15 +12,18 @@
 F32 = jnp.float32
 LO = 256
 VMEM_BYTES = 56 * 2**20
+TILE = 1024
+EARLY = 2048
+UNROLL = 16
 
 
 def outgoing_kernel(send_ref, hub_ref, feat_ref, out_ref, wide, picked, *, peers, rows, hubs):
     nodes = feat_ref.shape[0]
     block = rows + hubs
 
-    @pl.loop(0, nodes // 256)
+    @pl.loop(0, nodes // 512)
     def _(step):
-        at = pl.ds(pl.multiple_of(step * 256, 256), 256)
+        at = pl.ds(pl.multiple_of(step * 512, 512), 512)
         wide[at, :] = feat_ref[at, :].astype(F32)
 
     mine = jnp.concatenate([wide[pl.ds(hub_ref[j], 1), :] for j in range(hubs)], axis=0)
@@ -49,11 +52,10 @@
 
 def count_group(row, group, first, last):
     lanes = row.shape[1]
-    per = lanes // group
     high = lax.shift_right_arithmetic(row, 8)
     low = row & (LO - 1)
     shape = (2 * group, lanes)
-    lane_node = lax.broadcasted_iota(jnp.int32, shape, 1) // per
+    lane_node = lax.broadcasted_iota(jnp.int32, shape, 1) % group
     sub = lax.broadcasted_iota(jnp.int32, shape, 0)
     mine = jnp.where(lane_node == sub % group, jnp.broadcast_to(high, shape) - sub // group, -100).astype(jnp.int8)
     one = jnp.ones(shape, F8)
@@ -67,57 +69,65 @@
     return counts.reshape(last - first, group, LO)
 
 
-def fill_counts(counts, index_ref, base, tile, group, first, last, unroll):
+def group_rows(slot_ref, degree_ref, at, line, group):
+    lane_slot = lax.broadcasted_iota(jnp.int32, (8, 128), 1) // group
+    slot = lax.broadcasted_iota(jnp.int32, (8, 128), 0)
+    parts = []
+    for j in range(slot_ref.shape[0]):
+        lines = jnp.where(slot + 8 * j < degree_ref[pl.ds(line, 1), :], slot_ref[j, at], -1)
+        lines = pltpu.roll(lines, group, 1, stride=group, stride_axis=0)
+        turned = jnp.zeros((8, 128), jnp.int32)
+        for s in range(8):
+            one = jnp.broadcast_to(lines[s : s + 1], (8, 128))
+            turned = jnp.where(lane_slot == s, pltpu.roll(one, 0, 1, stride=group, stride_axis=0), turned)
+        parts.append(turned)
+    return jnp.concatenate(parts, axis=1)
+
+
+def fill_counts(counts, index_ref, base, tile, group, first, last):
     def pair(i, carry):
-        both = [count_group(index_ref[pl.ds(base + 2 * i + j, 1), :], group, first, last) for j in range(2)]
+        both = [count_group(index_ref[pl.ds(base + ((2 * i + j) ^ 7), 1), :], group, first, last) for j in range(2)]
         both = jnp.concatenate(both, axis=1).astype(F8)
         at = pl.ds(pl.multiple_of(i * 2 * group, 2 * group), 2 * group)
         for h in range(last - first):
             counts[at, h * LO : (h + 1) * LO] = both[h]
         return carry
 
-    lax.fori_loop(0, tile // (2 * group), pair, 0, unroll=unroll)
-
-
-def own_kernel(slot_ref, degree_ref, feat_ref, index_ref, table_ref, part_ref, counts, *, tile, early, group, fanout, own):
-    nodes, width = feat_ref.shape
-    lanes = group * fanout
-    half = nodes // 128 * 8
-
-    pick = lax.broadcasted_iota(jnp.int32, (fanout, lanes), 0) == lax.broadcasted_iota(jnp.int32, (fanout, lanes), 1) % fanout
-    pick = jnp.where(pick, 1.0, 0.0).astype(BF16)
-    slot = lax.broadcasted_iota(jnp.int32, (fanout, 128), 0)
-    sub = lax.broadcasted_iota(jnp.int32, (128, lanes), 0)
-    keep = sub % group == lax.broadcasted_iota(jnp.int32, (128, lanes), 1) // fanout
+    lax.fori_loop(0, tile // (2 * group), pair, 0, unroll=UNROLL)
+
+
+def own_kernel(
+    slot_ref, degree_ref, feat_ref, index_ref, table_ref, part_ref, counts, feat, table, index, sems, *, tile, early, group, own
+):
+    nodes = feat.shape[0]
+    fetch = pltpu.make_async_copy(feat_ref, feat, sems.at[0])
+    save_table = pltpu.make_async_copy(table, table_ref, sems.at[1])
+    save_index = pltpu.make_async_copy(index, index_ref, sems.at[2])
+    fetch.start()
 
     def relay(i, carry):
-        at = pl.multiple_of(i * 8, 8)
-        lines = jnp.concatenate([slot_ref[pl.ds(at + half * j, 8), :] for j in range(fanout // 8)], axis=0)
-        lines = jnp.where(slot < degree_ref[pl.ds(i, 1), :], lines, -1)
-        high = lax.shift_right_arithmetic(lines, 8).astype(F32).astype(BF16)
-        low = (lines & 255).astype(F32).astype(BF16)
-        turned = [
-            lax.dot_general(part, pick, (((0,), (0,)), ((), ())), preferred_element_type=F32) for part in (high, low)
-        ]
-        turned = jnp.where(keep, turned[0] * 256.0 + turned[1], 0.0)
-        rows = [jnp.sum(turned[g * group : (g + 1) * group], axis=0, keepdims=True) for g in range(128 // group)]
-        index_ref[pl.ds(pl.multiple_of(i * (128 // group), 128 // group), 128 // group), :] = jnp.concatenate(rows, axis=0).astype(
-            jnp.int32
-        )
+        index[pl.ds(pl.multiple_of(i * 8, 8), 8), :] = group_rows(slot_ref, degree_ref, i, i, group)
         return carry
 
-    lax.fori_loop(0, nodes // 128, relay, 0, unroll=2)
-
-    @pl.loop(0, nodes // 256)
+    lax.fori_loop(0, nodes // 128, relay, 0, unroll=8)
+    save_index.start()
+    fetch.wait()
+
+    @pl.loop(0, nodes // 512)
     def _(i):
-        at = pl.ds(pl.multiple_of(i * 256, 256), 256)
-        table_ref[at, :] = split(feat_ref[at, :])
+        at = pl.ds(pl.multiple_of(i * 512, 512), 512)
+        table[at, :] = split(feat[at, :])
+
+    save_table.start()
 
     @pl.loop(0, early // tile)
     def _(t):
-        fill_counts(counts, index_ref, t * (tile // group), tile, group, 0, own, 8)
-        total = jnp.dot(counts[...], table_ref[...], preferred_element_type=F32)
+        fill_counts(counts, index, t * (tile // group), tile, group, 0, own)
+        total = jnp.dot(counts[...], table[...], preferred_element_type=F32)
         part_ref[pl.ds(pl.multiple_of(t * tile, tile), tile), :] = joined(total)
+
+    save_index.wait()
+    save_table.wait()
 
 
 def layer_kernel(
@@ -127,10 +137,10 @@
     nodes, width = table_ref.shape[0], feat_ref.shape[1]
     step = pl.program_id(0)
     block = rows + hubs
+    copy = pltpu.make_async_copy(table_ref, table.at[pl.ds(0, nodes)], sem)
 
     @pl.when(step == 0)
     def _():
-        copy = pltpu.make_async_copy(table_ref, table.at[pl.ds(0, nodes)], sem)
         copy.start()
         wide[...] = halo_ref[...].astype(F32)
         hub_rows[...] = jnp.zeros_like(hub_rows)
@@ -142,7 +152,6 @@
             hub_rows[pl.ds(pl.multiple_of(i * hubs, 8), hubs), :] = wide[pl.ds(at + rows, hubs), :]
 
         table[nodes + peers * rows :, :] = split(hub_rows[...])
-        copy.wait()
 
     def finish(total):
         eye = lax.broadcasted_iota(jnp.int32, (128, 128), 0) == lax.broadcasted_iota(jnp.int32, (128, 128), 1)
@@ -158,13 +167,17 @@
 
     @pl.when(step < early // tile)
     def _():
-        fill_counts(counts, index_ref, 0, tile, group, own, highs, 8)
+        fill_counts(counts, index_ref, 0, tile, group, own, highs)
         total = jnp.dot(counts[:, : (highs - own) * LO], table[own * LO :, :], preferred_element_type=F32)
         finish(joined(total) + part_ref[...])
 
+    @pl.when(step == early // tile)
+    def _():
+        copy.wait()
+
     @pl.when(step >= early // tile)
     def _():
-        fill_counts(counts, index_ref, 0, tile, group, 0, highs, 8)
+        fill_counts(counts, index_ref, 0, tile, group, 0, highs)
         finish(joined(jnp.dot(counts[...], table[...], preferred_element_type=F32)))
 
 
@@ -178,12 +191,14 @@
     own = nodes // LO
     highs = -(-(nodes + peers * block) // (2 * LO)) * 2
     hub_space = highs * LO - nodes - peers * rows
-    tile = 512
-    early = 2048
+    tile = TILE
+    early = EARLY
     smem = pl.BlockSpec(memory_space=pltpu.SMEM)
     vmem = pl.BlockSpec(memory_space=pltpu.VMEM)
     params = pltpu.CompilerParams(vmem_limit_bytes=VMEM_BYTES)
 
+    lines = neighbors.T.reshape(fanout // 8, 8, nodes // 128, 128).transpose(0, 2, 1, 3)
+    degrees = degree.reshape(nodes // 128, 128)
     outgoing = pl.pallas_call(
         functools.partial(outgoing_kernel, peers=peers, rows=rows, hubs=hubs),
         in_specs=[smem, smem, vmem],
@@ -196,22 +211,35 @@
     halo = lax.all_to_all(outgoing.reshape(peers, block, width), "node", split_axis=0, concat_axis=0, tiled=True)
     halo = halo.reshape(peers * block, width)
 
-    lines = neighbors.T.reshape(fanout // 8, 8, nodes // 128, 128).transpose(0, 2, 1, 3).reshape(-1, 128)
-    counts_of = degree.reshape(nodes // 128, 128)
     index, table, part = pl.pallas_call(
-        functools.partial(own_kernel, tile=tile, early=early, group=group, fanout=fanout, own=own),
-        in_specs=[vmem, vmem, vmem],
-        out_specs=[vmem, vmem, vmem],
+        functools.partial(own_kernel, tile=tile, early=early, group=group, own=own),
+        grid=(1,),
+        in_specs=[
+            pl.BlockSpec((fanout // 8, nodes // 128, 8, 128), lambda i: (0, 0, 0, 0)),
+            pl.BlockSpec((nodes // 128, 128), lambda i: (0, 0)),
+            pl.BlockSpec(memory_space=pl.ANY),
+        ],
+        out_specs=[
+            pl.BlockSpec(memory_space=pl.ANY),
+            pl.BlockSpec(memory_space=pl.ANY),
+            pl.BlockSpec((early, width), lambda i: (0, 0)),
+        ],
         out_shape=[
             jax.ShapeDtypeStruct((nodes // group, group * fanout), jnp.int32),
             jax.ShapeDtypeStruct((nodes, 2 * width), F8),
             jax.ShapeDtypeStruct((early, width), F32),
         ],
-        scratch_shapes=[pltpu.VMEM((tile, own * LO), F8)],
+        scratch_shapes=[
+            pltpu.VMEM((tile, own * LO), F8),
+            pltpu.VMEM((nodes, width), BF16),
+            pltpu.VMEM((nodes, 2 * width), F8),
+            pltpu.VMEM((nodes // group, group * fanout), jnp.int32),
+            pltpu.SemaphoreType.DMA((3,)),
+        ],
         compiler_params=params,
         cost_estimate=pl.CostEstimate(flops=30_000_000_000, bytes_accessed=6_000_000, transcendentals=0),
         name="own_part",
-    )(lines, counts_of, features)
+    )(lines, degrees, features)
 
     whole = lambda *shape: pl.BlockSpec(shape, lambda i: (0,) * len(shape))
     last_early = early // tile - 1
@@ -242,7 +270,7 @@
         ],
         compiler_params=params,
         name="sage_layer",
-    )(index, counts_of, part, features, halo, table, w_self, w_neigh, bias.reshape(1, width))
+    )(index, degrees, part, features, halo, table, w_self, w_neigh, bias.reshape(1, width))
 
 
 def solution(mesh):

time: 89.9 us -> 76.1 us (0.85)
  Pallas kernels: 81.4 us -> 67.5 us
    pallas_call x1, Pallas kernels: 23.2 us -> 15.3 us  [local(): pl.pallas_call(functools.partial(own_kernel, tile=tile, early=early, grou...]
    pallas_call x1, Pallas kernels: 53.6 us -> 47.7 us  [local(): pl.pallas_call(functools.partial(layer_kernel, tile=tile, early=early, gr...]
  transfers between devices with their start and end apart: 1 -> 1, of which waited for: 0 -> 0; matrix products, arithmetic and copies ran while one was open for 0% -> 0% of each run, Pallas kernels for 26% -> 20%
where the time goes in v3:
time: 76.1 us; the launch traced here: 75.8 us
  Pallas kernels  67.5 us (89%)
  starting transfers between devices  7.39 us (10%)
  local copies, waits for them, and re-layouts  0.8 us (1%)
    pallas_call x1, Pallas kernels, local(): pl.pallas_call(functools.partial(layer_kernel, tile=tile, early=early, gr...  47.7 us
    pallas_call x1, Pallas kernels, local(): pl.pallas_call(functools.partial(own_kernel, tile=tile, early=early, grou...  15.3 us
    all_to_all x1, starting transfers between devices, local(): lax.all_to_all(outgoing.reshape(peers, block, width), 'node', split_axis=...  7.39 us
    pallas_call x1, Pallas kernels, local(): pl.pallas_call(functools.partial(outgoing_kernel, peers=peers, rows=rows,...  4.5 us
  transfers between devices with their start and end apart: 1, of which 0 were waited for; matrix products, arithmetic and copies ran while one was open for 0% of the time, Pallas kernels for 20%

profile of v3, /device:TPU:0, one launch (start us, length us, event | category | flops | bytes accessed | tf_op | source)
XLA Modules:
  0.0 75.8 jit_solution(14523683145642369690)
XLA Ops:
  0.0 4.5 %outgoing_rows.1 = bf16[2176,128]{1,0:T(8,128)(2,1)} custom-call(s32[2048]{0:T(1024)} %bitcast.15, s32[8]{0:T(128)} %bitcast.16, bf16[8192,128]{1,0:T(8,128)(2,1)} %feat_ref.5), custom_call_target="tpu_custom_call" | custom-call | tf_op jit(solution)/shard_map/outgoing_rows/pallas_call | solution.py:202
  4.5 7.4 %all-to-all-start = ((bf16[16,136,128]{2,1,0:T(8,128)(2,1)}), bf16[16,136,128]{2,1,0:T(8,128)(2,1)S(1)}, u32[]{:S(2)}, u32[]{:S(2)}) async-start(bf16[16,136,128]{2,1,0:T(8,128)(2,1)} %bitcast.12), calls=%async_computation | async-start | bytes 1114112 | tf_op jit(solution)/shard_map/all_to_all | solution.py:211
  11.9 15.3 %own_part.1 = (s32[512,256]{1,0:T(8,128)}, f8e4m3fn[8192,256]{1,0:T(32,128)(4,1)}, f32[2048,128]{1,0:T(8,128)}) custom-call(s32[2,64,8,128]{3,2,1,0:T(8,128)} %bitcast.18, s32[64,128]{1,0:T(8,128)} %bitcast.13, bf16[8192,128]{1,0:T(8,128)(2,1)} %feat_ref.5), custom_call_target="tpu_custom_call" | custom-call | flops 30000001024 | bytes 6000000 | tf_op jit(solution)/shard_map/own_part/pallas_call | solution.py:214
  27.2 0.0 all-to-all-done
  27.2 0.0 copy-start
  27.2 0.8 %copy-done = bf16[16,136,128]{2,1,0:T(8,128)(2,1)} copy-done((bf16[16,136,128]{2,1,0:T(8,128)(2,1)}, bf16[16,136,128]{2,1,0:T(8,128)(2,1)S(1)}, u32[]{:S(2)}) %copy-start) | copy-done | bytes 557080
  28.0 47.7 %sage_layer.1 = bf16[8192,128]{1,0:T(8,128)(2,1)} custom-call(s32[512,256]{1,0:T(8,128)} %get-tuple-element.8.index_ref, s32[64,128]{1,0:T(8,128)} %bitcast.14, f32[2048,128]{1,0:T(8,128)} %get-tuple-element.9.part_ref, bf16[8192,128]{1,0:T(8,128)(2,1)} %feat_ref.5, bf16[2176,128]{1,0:T(8,128)(2,1)} %bitcast.11, ...), custom_call_target="tpu_custom_call" | custom-call | tf_op jit(solution)/shard_map/sage_layer/pallas_call | solution.py:246
Async XLA Ops:
  4.5 22.7 %all-to-all-start = ((bf16[16,136,128]{2,1,0:T(8,128)(2,1)}), bf16[16,136,128]{2,1,0:T(8,128)(2,1)S(1)}, u32[]{:S(2)}, u32[]{:S(2)}) async-start(bf16[16,136,128]{2,1,0:T(8,128)(2,1)} %bitcast.12), calls=%async_computation | async-start | bytes 1114112 | tf_op jit(solution)/shard_map/all_to_all | solution.py:211
  27.2 0.8 %copy-start = (bf16[16,136,128]{2,1,0:T(8,128)(2,1)}, bf16[16,136,128]{2,1,0:T(8,128)(2,1)S(1)}, u32[]{:S(2)}) copy-start(bf16[16,136,128]{2,1,0:T(8,128)(2,1)S(1)} %all-to-all-done) | copy-start | bytes 1671172

commit v4 on v3

--- a/solution.py
+++ b/solution.py
@@ -11,7 +11,7 @@
 BF16 = jnp.bfloat16
 F32 = jnp.float32
 LO = 256
-VMEM_BYTES = 56 * 2**20
+VMEM_BYTES = 255 * 2**18
 TILE = 1024
 EARLY = 2048
 UNROLL = 16
@@ -28,12 +28,17 @@
 
     mine = jnp.concatenate([wide[pl.ds(hub_ref[j], 1), :] for j in range(hubs)], axis=0)
 
-    @pl.loop(0, peers)
-    def _(peer):
-        to = picked.at[pl.ds(pl.multiple_of(peer * block, 8), block)]
+    def gather(peer):
+        to = picked.at[pl.ds(peer * block, block)]
         for c in range(rows):
             to[c : c + 1, :] = wide[pl.ds(send_ref[peer * rows + c], 1), :]
         to[rows:, :] = mine
+
+    if peers <= 16:
+        for peer in range(peers):
+            gather(peer)
+    else:
+        pl.loop(0, peers)(gather)
 
     out_ref[...] = picked[...].astype(BF16)
 
@@ -84,32 +89,39 @@
     return jnp.concatenate(parts, axis=1)
 
 
-def fill_counts(counts, index_ref, base, tile, group, first, last):
+def fill_counts(counts, index_ref, base, tile, group, first, last, beside=None):
     def pair(i, carry):
         both = [count_group(index_ref[pl.ds(base + ((2 * i + j) ^ 7), 1), :], group, first, last) for j in range(2)]
         both = jnp.concatenate(both, axis=1).astype(F8)
         at = pl.ds(pl.multiple_of(i * 2 * group, 2 * group), 2 * group)
         for h in range(last - first):
             counts[at, h * LO : (h + 1) * LO] = both[h]
+        if beside is not None:
+            beside(i)
         return carry
 
     lax.fori_loop(0, tile // (2 * group), pair, 0, unroll=UNROLL)
 
 
 def own_kernel(
-    slot_ref, degree_ref, feat_ref, index_ref, table_ref, part_ref, counts, feat, table, index, sems, *, tile, early, group, own
+    slot_ref, degree_ref, feat_ref, index_ref, table_ref, part_ref,
+    counts, feat, table, index, later, sems, *, tile, early, group, own
 ):
     nodes = feat.shape[0]
+    lines = nodes // 128
+    early_lines = early // 128
+    last = early // tile - 1
     fetch = pltpu.make_async_copy(feat_ref, feat, sems.at[0])
     save_table = pltpu.make_async_copy(table, table_ref, sems.at[1])
-    save_index = pltpu.make_async_copy(index, index_ref, sems.at[2])
+    save_index = pltpu.make_async_copy(index, index_ref.at[pl.ds(0, early // group)], sems.at[2])
+    save_later = pltpu.make_async_copy(later, index_ref.at[pl.ds(early // group, (nodes - early) // group)], sems.at[3])
     fetch.start()
 
     def relay(i, carry):
         index[pl.ds(pl.multiple_of(i * 8, 8), 8), :] = group_rows(slot_ref, degree_ref, i, i, group)
         return carry
 
-    lax.fori_loop(0, nodes // 128, relay, 0, unroll=8)
+    lax.fori_loop(0, early_lines, relay, 0, unroll=8)
     save_index.start()
     fetch.wait()
 
@@ -120,32 +132,48 @@
 
     save_table.start()
 
-    @pl.loop(0, early // tile)
+    @pl.loop(0, last + 1)
     def _(t):
-        fill_counts(counts, index, t * (tile // group), tile, group, 0, own)
+        def relay_later(i):
+            line = jnp.minimum(t * (tile // (2 * group)) + i, lines - early_lines - 1)
+            rows = group_rows(slot_ref, degree_ref, early_lines + line, early_lines + line, group)
+            later[pl.ds(pl.multiple_of(line * 8, 8), 8), :] = rows
+
+        fill_counts(counts, index, t * (tile // group), tile, group, 0, own, relay_later)
+
+        @pl.when(t == last)
+        def _():
+            save_later.start()
+
         total = jnp.dot(counts[...], table[...], preferred_element_type=F32)
         part_ref[pl.ds(pl.multiple_of(t * tile, tile), tile), :] = joined(total)
 
     save_index.wait()
     save_table.wait()
+    save_later.wait()
 
 
 def layer_kernel(
     index_ref, degree_ref, part_ref, feat_ref, halo_ref, table_ref, self_ref, neigh_ref, bias_ref, out_ref,
-    table, counts, wide, hub_rows, sem, *, tile, early, group, peers, rows, hubs, own, highs
+    table, counts, halo, wide, hub_rows, sems, *, tile, early, group, peers, rows, hubs, own, highs
 ):
     nodes, width = table_ref.shape[0], feat_ref.shape[1]
     step = pl.program_id(0)
     block = rows + hubs
-    copy = pltpu.make_async_copy(table_ref, table.at[pl.ds(0, nodes)], sem)
+    own_copy = pltpu.make_async_copy(table_ref, table.at[pl.ds(0, nodes)], sems.at[0])
+    halo_copy = pltpu.make_async_copy(halo_ref, halo, sems.at[1])
 
     @pl.when(step == 0)
     def _():
-        copy.start()
-        wide[...] = halo_ref[...].astype(F32)
+        halo_copy.start()
+        own_copy.start()
+
+    def add_halo():
+        halo_copy.wait()
+        wide[...] = halo[...].astype(F32)
         hub_rows[...] = jnp.zeros_like(hub_rows)
 
-        @pl.loop(0, peers)
+        @pl.loop(0, peers, unroll=4)
         def _(i):
             at = pl.multiple_of(i * block, 8)
             table[pl.ds(pl.multiple_of(nodes + i * rows, 32), rows), :] = split(wide[pl.ds(at, rows), :])
@@ -168,12 +196,13 @@
     @pl.when(step < early // tile)
     def _():
         fill_counts(counts, index_ref, 0, tile, group, own, highs)
+        pl.when(step == 0)(add_halo)
         total = jnp.dot(counts[:, : (highs - own) * LO], table[own * LO :, :], preferred_element_type=F32)
         finish(joined(total) + part_ref[...])
 
     @pl.when(step == early // tile)
     def _():
-        copy.wait()
+        own_copy.wait()
 
     @pl.when(step >= early // tile)
     def _():
@@ -233,8 +262,9 @@
             pltpu.VMEM((tile, own * LO), F8),
             pltpu.VMEM((nodes, width), BF16),
             pltpu.VMEM((nodes, 2 * width), F8),
-            pltpu.VMEM((nodes // group, group * fanout), jnp.int32),
-            pltpu.SemaphoreType.DMA((3,)),
+            pltpu.VMEM((early // group, group * fanout), jnp.int32),
+            pltpu.VMEM(((nodes - early) // group, group * fanout), jnp.int32),
+            pltpu.SemaphoreType.DMA((4,)),
         ],
         compiler_params=params,
         cost_estimate=pl.CostEstimate(flops=30_000_000_000, bytes_accessed=6_000_000, transcendentals=0),
@@ -253,7 +283,7 @@
             whole(nodes // 128, 128),
             pl.BlockSpec((tile, width), lambda i: (jnp.minimum(i, last_early), 0)),
             pl.BlockSpec((tile, width), lambda i: (i, 0)),
-            whole(peers * block, width),
+            pl.BlockSpec(memory_space=pl.ANY),
             pl.BlockSpec(memory_space=pl.ANY),
             whole(width, width),
             whole(width, width),
@@ -264,9 +294,10 @@
         scratch_shapes=[
             pltpu.VMEM((highs * LO, 2 * width), F8),
             pltpu.VMEM((tile, highs * LO), F8),
+            pltpu.VMEM((peers * block, width), BF16),
             pltpu.VMEM((peers * block, width), F32),
             pltpu.VMEM((hub_space, width), F32),
-            pltpu.SemaphoreType.DMA,
+            pltpu.SemaphoreType.DMA((2,)),
         ],
         compiler_params=params,
         name="sage_layer",

time: 76.1 us -> 74.4 us (0.978)
  Pallas kernels: 67.5 us -> 66.6 us
  local copies, waits for them, and re-layouts: 0.8 us -> 0 us
    unnamed x2 -> x0, local copies, waits for them, and re-layouts: 0.8 us -> none
  transfers between devices with their start and end apart: 1 -> 1, of which waited for: 0 -> 0; matrix products, arithmetic and copies ran while one was open for 0% -> 0% of each run, Pallas kernels for 20% -> 21%
where the time goes in v4:
time: 74.4 us; the launch traced here: 74.1 us
  Pallas kernels  66.6 us (90%)
  starting transfers between devices  7.43 us (10%)
    pallas_call x1, Pallas kernels, local(): pl.pallas_call(functools.partial(layer_kernel, tile=tile, early=early, gr...  47.5 us
    pallas_call x1, Pallas kernels, local(): pl.pallas_call(functools.partial(own_kernel, tile=tile, early=early, grou...  15.3 us
    all_to_all x1, starting transfers between devices, local(): lax.all_to_all(outgoing.reshape(peers, block, width), 'node', split_axis=...  7.43 us
    pallas_call x1, Pallas kernels, local(): pl.pallas_call(functools.partial(outgoing_kernel, peers=peers, rows=rows,...  3.88 us
  transfers between devices with their start and end apart: 1, of which 0 were waited for; matrix products, arithmetic and copies ran while one was open for 0% of the time, Pallas kernels for 21%

profile of v4, /device:TPU:0, one launch (start us, length us, event | category | flops | bytes accessed | tf_op | source)
XLA Modules:
  0.0 74.1 jit_solution(10995848146220671844)
XLA Ops:
  0.0 3.9 %outgoing_rows.1 = bf16[2176,128]{1,0:T(8,128)(2,1)} custom-call(s32[2048]{0:T(1024)} %bitcast.14, s32[8]{0:T(128)} %bitcast.15, bf16[8192,128]{1,0:T(8,128)(2,1)} %feat_ref.5), custom_call_target="tpu_custom_call" | custom-call | tf_op jit(solution)/shard_map/outgoing_rows/pallas_call | solution.py:231
  3.9 7.4 %all-to-all-start = ((bf16[16,136,128]{2,1,0:T(8,128)(2,1)}), bf16[16,136,128]{2,1,0:T(8,128)(2,1)}, u32[]{:S(2)}, u32[]{:S(2)}) async-start(bf16[16,136,128]{2,1,0:T(8,128)(2,1)} %bitcast.11), calls=%async_computation | async-start | bytes 1114112 | tf_op jit(solution)/shard_map/all_to_all | solution.py:240
  11.3 15.3 %own_part.1 = (s32[512,256]{1,0:T(8,128)}, f8e4m3fn[8192,256]{1,0:T(32,128)(4,1)}, f32[2048,128]{1,0:T(8,128)}) custom-call(s32[2,64,8,128]{3,2,1,0:T(8,128)} %bitcast.17, s32[64,128]{1,0:T(8,128)} %bitcast.12, bf16[8192,128]{1,0:T(8,128)(2,1)} %feat_ref.5), custom_call_target="tpu_custom_call" | custom-call | flops 30000001024 | bytes 6000000 | tf_op jit(solution)/shard_map/own_part/pallas_call | solution.py:243
  26.6 0.0 all-to-all-done
  26.6 47.5 %sage_layer.1 = bf16[8192,128]{1,0:T(8,128)(2,1)} custom-call(s32[512,256]{1,0:T(8,128)} %get-tuple-element.8.index_ref, s32[64,128]{1,0:T(8,128)} %bitcast.13, f32[2048,128]{1,0:T(8,128)} %get-tuple-element.9.part_ref, bf16[8192,128]{1,0:T(8,128)(2,1)} %feat_ref.5, bf16[2176,128]{1,0:T(8,128)(2,1)} %bitcast.7.halo_ref, ...), custom_call_target="tpu_custom_call" | custom-call | tf_op jit(solution)/shard_map/sage_layer/pallas_call | solution.py:276
Async XLA Ops:
  3.9 22.7 %all-to-all-start = ((bf16[16,136,128]{2,1,0:T(8,128)(2,1)}), bf16[16,136,128]{2,1,0:T(8,128)(2,1)}, u32[]{:S(2)}, u32[]{:S(2)}) async-start(bf16[16,136,128]{2,1,0:T(8,128)(2,1)} %bitcast.11), calls=%async_computation | async-start | bytes 1114112 | tf_op jit(solution)/shard_map/all_to_all | solution.py:240

commit v5 on v4

--- a/solution.py
+++ b/solution.py
@@ -43,16 +43,31 @@
     out_ref[...] = picked[...].astype(BF16)
 
 
-def split(values):
-    scaled = values.astype(F32) * 64.0
+def largest(values):
+    return jnp.max(jnp.abs(values.astype(F32)).reshape(-1, 8, values.shape[1]), axis=0)
+
+
+def fit(most):
+    most = jnp.broadcast_to(jnp.max(jnp.max(most, axis=0, keepdims=True), axis=1, keepdims=True), most.shape)
+    scale = jnp.ones_like(most)
+    inverse = jnp.ones_like(most)
+    for bits in (32, 16, 8, 4, 2, 1):
+        fits = most * (scale * 2.0**bits) <= 448.0
+        scale = jnp.where(fits, scale * 2.0**bits, scale)
+        inverse = jnp.where(fits, inverse * 2.0**-bits, inverse)
+    return scale, inverse
+
+
+def split(values, scale):
+    scaled = values.astype(F32) * scale
     high = scaled.astype(F8)
     low = ((scaled - high.astype(F32)) * 16.0).astype(F8)
     return jnp.concatenate([high, low], axis=1)
 
 
-def joined(total):
+def joined(total, inverse):
     width = total.shape[1] // 2
-    return total[:, :width] * (1.0 / 64.0) + total[:, width:] * (1.0 / 1024.0)
+    return (total[:, :width] + total[:, width:] * (1.0 / 16.0)) * inverse
 
 
 def count_group(row, group, first, last):
@@ -104,7 +119,7 @@
 
 
 def own_kernel(
-    slot_ref, degree_ref, feat_ref, index_ref, table_ref, part_ref,
+    slot_ref, degree_ref, feat_ref, index_ref, table_ref, part_ref, inverse_ref,
     counts, feat, table, index, later, sems, *, tile, early, group, own
 ):
     nodes = feat.shape[0]
@@ -125,10 +140,15 @@
     save_index.start()
     fetch.wait()
 
+    def most_of(i, most):
+        return jnp.maximum(most, largest(feat[pl.ds(pl.multiple_of(i * 512, 512), 512), :]))
+
+    scale, inverse_ref[...] = fit(lax.fori_loop(0, nodes // 512, most_of, jnp.zeros(inverse_ref.shape, F32)))
+
     @pl.loop(0, nodes // 512)
     def _(i):
         at = pl.ds(pl.multiple_of(i * 512, 512), 512)
-        table[at, :] = split(feat[at, :])
+        table[at, :] = split(feat[at, :], scale[:1])
 
     save_table.start()
 
@@ -146,7 +166,7 @@
             save_later.start()
 
         total = jnp.dot(counts[...], table[...], preferred_element_type=F32)
-        part_ref[pl.ds(pl.multiple_of(t * tile, tile), tile), :] = joined(total)
+        part_ref[pl.ds(pl.multiple_of(t * tile, tile), tile), :] = joined(total, inverse_ref[:1])
 
     save_index.wait()
     save_table.wait()
@@ -154,8 +174,8 @@
 
 
 def layer_kernel(
-    index_ref, degree_ref, part_ref, feat_ref, halo_ref, table_ref, self_ref, neigh_ref, bias_ref, out_ref,
-    table, counts, halo, wide, hub_rows, sems, *, tile, early, group, peers, rows, hubs, own, highs
+    index_ref, degree_ref, part_ref, own_inverse, feat_ref, halo_ref, table_ref, self_ref, neigh_ref, bias_ref, out_ref,
+    table, counts, halo_inverse, halo, wide, hub_rows, sems, *, tile, early, group, peers, rows, hubs, own, highs
 ):
     nodes, width = table_ref.shape[0], feat_ref.shape[1]
     step = pl.program_id(0)
@@ -171,15 +191,16 @@
     def add_halo():
         halo_copy.wait()
         wide[...] = halo[...].astype(F32)
+        scale, halo_inverse[...] = fit(largest(wide[...]))
         hub_rows[...] = jnp.zeros_like(hub_rows)
 
         @pl.loop(0, peers, unroll=4)
         def _(i):
             at = pl.multiple_of(i * block, 8)
-            table[pl.ds(pl.multiple_of(nodes + i * rows, 32), rows), :] = split(wide[pl.ds(at, rows), :])
+            table[pl.ds(pl.multiple_of(nodes + i * rows, 32), rows), :] = split(wide[pl.ds(at, rows), :], scale[:1])
             hub_rows[pl.ds(pl.multiple_of(i * hubs, 8), hubs), :] = wide[pl.ds(at + rows, hubs), :]
 
-        table[nodes + peers * rows :, :] = split(hub_rows[...])
+        table[nodes + peers * rows :, :] = split(hub_rows[...], scale[:1])
 
     def finish(total):
         eye = lax.broadcasted_iota(jnp.int32, (128, 128), 0) == lax.broadcasted_iota(jnp.int32, (128, 128), 1)
@@ -198,7 +219,7 @@
         fill_counts(counts, index_ref, 0, tile, group, own, highs)
         pl.when(step == 0)(add_halo)
         total = jnp.dot(counts[:, : (highs - own) * LO], table[own * LO :, :], preferred_element_type=F32)
-        finish(joined(total) + part_ref[...])
+        finish(joined(total, halo_inverse[:1]) + part_ref[...])
 
     @pl.when(step == early // tile)
     def _():
@@ -207,7 +228,10 @@
     @pl.when(step >= early // tile)
     def _():
         fill_counts(counts, index_ref, 0, tile, group, 0, highs)
-        finish(joined(jnp.dot(counts[...], table[...], preferred_element_type=F32)))
+        total = jnp.dot(counts[:, own * LO :], table[own * LO :, :], preferred_element_type=F32)
+        total = joined(total, halo_inverse[:1])
+        rest = jnp.dot(counts[:, : own * LO], table[: own * LO, :], preferred_element_type=F32)
+        finish(total + joined(rest, own_inverse[:1]))
 
 
 def local(features, neighbors, degree, send_list, hub_rows, w_self, w_neigh, bias):
@@ -240,7 +264,7 @@
     halo = lax.all_to_all(outgoing.reshape(peers, block, width), "node", split_axis=0, concat_axis=0, tiled=True)
     halo = halo.reshape(peers * block, width)
 
-    index, table, part = pl.pallas_call(
+    index, table, part, inverse = pl.pallas_call(
         functools.partial(own_kernel, tile=tile, early=early, group=group, own=own),
         grid=(1,),
         in_specs=[
@@ -252,11 +276,13 @@
             pl.BlockSpec(memory_space=pl.ANY),
             pl.BlockSpec(memory_space=pl.ANY),
             pl.BlockSpec((early, width), lambda i: (0, 0)),
+            pl.BlockSpec((8, width), lambda i: (0, 0)),
         ],
         out_shape=[
             jax.ShapeDtypeStruct((nodes // group, group * fanout), jnp.int32),
             jax.ShapeDtypeStruct((nodes, 2 * width), F8),
             jax.ShapeDtypeStruct((early, width), F32),
+            jax.ShapeDtypeStruct((8, width), F32),
         ],
         scratch_shapes=[
             pltpu.VMEM((tile, own * LO), F8),
@@ -282,6 +308,7 @@
             pl.BlockSpec((tile // group, group * fanout), lambda i: (i, 0)),
             whole(nodes // 128, 128),
             pl.BlockSpec((tile, width), lambda i: (jnp.minimum(i, last_early), 0)),
+            whole(8, width),
             pl.BlockSpec((tile, width), lambda i: (i, 0)),
             pl.BlockSpec(memory_space=pl.ANY),
             pl.BlockSpec(memory_space=pl.ANY),
@@ -294,6 +321,7 @@
         scratch_shapes=[
             pltpu.VMEM((highs * LO, 2 * width), F8),
             pltpu.VMEM((tile, highs * LO), F8),
+            pltpu.VMEM((8, width), F32),
             pltpu.VMEM((peers * block, width), BF16),
             pltpu.VMEM((peers * block, width), F32),
             pltpu.VMEM((hub_space, width), F32),
@@ -301,7 +329,7 @@
         ],
         compiler_params=params,
         name="sage_layer",
-    )(index, degrees, part, features, halo, table, w_self, w_neigh, bias.reshape(1, width))
+    )(index, degrees, part, inverse, features, halo, table, w_self, w_neigh, bias.reshape(1, width))
 
 
 def solution(mesh):

time: 74.4 us -> 75.1 us (level)
  Pallas kernels: 66.6 us -> 67.4 us
where the time goes in v5:
time: 75.1 us; the launch traced here: 74.8 us
  Pallas kernels  67.4 us (90%)
  starting transfers between devices  7.43 us (10%)
    pallas_call x1, Pallas kernels, local(): pl.pallas_call(functools.partial(layer_kernel, tile=tile, early=early, gr...  47.7 us
    pallas_call x1, Pallas kernels, local(): pl.pallas_call(functools.partial(own_kernel, tile=tile, early=early, grou...  15.7 us
    all_to_all x1, starting transfers between devices, local(): lax.all_to_all(outgoing.reshape(peers, block, width), 'node', split_axis=...  7.43 us
    pallas_call x1, Pallas kernels, local(): pl.pallas_call(functools.partial(outgoing_kernel, peers=peers, rows=rows,...  3.88 us
  transfers between devices with their start and end apart: 1, of which 0 were waited for; matrix products, arithmetic and copies ran while one was open for 0% of the time, Pallas kernels for 21%

profile of v5, /device:TPU:0, one launch (start us, length us, event | category | flops | bytes accessed | tf_op | source)
XLA Modules:
  0.0 74.8 jit_solution(12805650454672109680)
XLA Ops:
  0.0 3.9 %outgoing_rows.1 = bf16[2176,128]{1,0:T(8,128)(2,1)} custom-call(s32[2048]{0:T(1024)} %bitcast.14, s32[8]{0:T(128)} %bitcast.15, bf16[8192,128]{1,0:T(8,128)(2,1)} %feat_ref.5), custom_call_target="tpu_custom_call" | custom-call | tf_op jit(solution)/shard_map/outgoing_rows/pallas_call | solution.py:255
  3.9 7.4 %all-to-all-start = ((bf16[16,136,128]{2,1,0:T(8,128)(2,1)}), bf16[16,136,128]{2,1,0:T(8,128)(2,1)}, u32[]{:S(2)}, u32[]{:S(2)}) async-start(bf16[16,136,128]{2,1,0:T(8,128)(2,1)} %bitcast.11), calls=%async_computation | async-start | bytes 1114112 | tf_op jit(solution)/shard_map/all_to_all | solution.py:264
  11.3 15.7 %own_part.1 = (s32[512,256]{1,0:T(8,128)}, f8e4m3fn[8192,256]{1,0:T(32,128)(4,1)}, f32[2048,128]{1,0:T(8,128)}, f32[8,128]{1,0:T(8,128)}) custom-call(s32[2,64,8,128]{3,2,1,0:T(8,128)} %bitcast.17, s32[64,128]{1,0:T(8,128)} %bitcast.12, bf16[8192,128]{1,0:T(8,128)(2,1)} %feat_ref.5), custom_call_target="tpu_custom_call" | custom-call | flops 30000001024 | bytes 6000000 | tf_op jit(solution)/shard_map/own_part/pallas_call | solution.py:267
  27.1 0.0 all-to-all-done
  27.1 47.7 %sage_layer.1 = bf16[8192,128]{1,0:T(8,128)(2,1)} custom-call(s32[512,256]{1,0:T(8,128)} %get-tuple-element.9.index_ref, s32[64,128]{1,0:T(8,128)} %bitcast.13, f32[2048,128]{1,0:T(8,128)} %get-tuple-element.10.part_ref, f32[8,128]{1,0:T(8,128)} %get-tuple-element.11.own_inverse, bf16[8192,128]{1,0:T(8,128)(2,1)} %feat_ref.5, ...), custom_call_target="tpu_custom_call" | custom-call | tf_op jit(solution)/shard_map/sage_layer/pallas_call | solution.py:302
Async XLA Ops:
  3.9 23.2 %all-to-all-start = ((bf16[16,136,128]{2,1,0:T(8,128)(2,1)}), bf16[16,136,128]{2,1,0:T(8,128)(2,1)}, u32[]{:S(2)}, u32[]{:S(2)}) async-start(bf16[16,136,128]{2,1,0:T(8,128)(2,1)} %bitcast.11), calls=%async_computation | async-start | bytes 1114112 | tf_op jit(solution)/shard_map/all_to_all | solution.py:264

commit v6 on v5

--- a/solution.py
+++ b/solution.py
@@ -17,14 +17,17 @@
 UNROLL = 16
 
 
-def outgoing_kernel(send_ref, hub_ref, feat_ref, out_ref, wide, picked, *, peers, rows, hubs):
+def outgoing_kernel(send_ref, hub_ref, feat_ref, out_ref, most_ref, wide, picked, *, peers, rows, hubs):
     nodes = feat_ref.shape[0]
     block = rows + hubs
 
-    @pl.loop(0, nodes // 512)
-    def _(step):
+    def widen(step, most):
         at = pl.ds(pl.multiple_of(step * 512, 512), 512)
-        wide[at, :] = feat_ref[at, :].astype(F32)
+        values = feat_ref[at, :].astype(F32)
+        wide[at, :] = values
+        return jnp.maximum(most, largest(values))
+
+    most_ref[...] = lax.fori_loop(0, nodes // 512, widen, jnp.zeros(most_ref.shape, F32))
 
     mine = jnp.concatenate([wide[pl.ds(hub_ref[j], 1), :] for j in range(hubs)], axis=0)
 
@@ -119,7 +122,7 @@
 
 
 def own_kernel(
-    slot_ref, degree_ref, feat_ref, index_ref, table_ref, part_ref, inverse_ref,
+    slot_ref, degree_ref, most_ref, feat_ref, index_ref, table_ref, part_ref, inverse_ref,
     counts, feat, table, index, later, sems, *, tile, early, group, own
 ):
     nodes = feat.shape[0]
@@ -140,10 +143,7 @@
     save_index.start()
     fetch.wait()
 
-    def most_of(i, most):
-        return jnp.maximum(most, largest(feat[pl.ds(pl.multiple_of(i * 512, 512), 512), :]))
-
-    scale, inverse_ref[...] = fit(lax.fori_loop(0, nodes // 512, most_of, jnp.zeros(inverse_ref.shape, F32)))
+    scale, inverse_ref[...] = fit(most_ref[...])
 
     @pl.loop(0, nodes // 512)
     def _(i):
@@ -252,11 +252,11 @@
 
     lines = neighbors.T.reshape(fanout // 8, 8, nodes // 128, 128).transpose(0, 2, 1, 3)
     degrees = degree.reshape(nodes // 128, 128)
-    outgoing = pl.pallas_call(
+    outgoing, most = pl.pallas_call(
         functools.partial(outgoing_kernel, peers=peers, rows=rows, hubs=hubs),
         in_specs=[smem, smem, vmem],
-        out_specs=vmem,
-        out_shape=jax.ShapeDtypeStruct((peers * block, width), BF16),
+        out_specs=[vmem, vmem],
+        out_shape=[jax.ShapeDtypeStruct((peers * block, width), BF16), jax.ShapeDtypeStruct((8, width), F32)],
         scratch_shapes=[pltpu.VMEM((nodes, width), F32), pltpu.VMEM((peers * block, width), F32)],
         compiler_params=params,
         name="outgoing_rows",
@@ -270,6 +270,7 @@
         in_specs=[
             pl.BlockSpec((fanout // 8, nodes // 128, 8, 128), lambda i: (0, 0, 0, 0)),
             pl.BlockSpec((nodes // 128, 128), lambda i: (0, 0)),
+            pl.BlockSpec((8, width), lambda i: (0, 0)),
             pl.BlockSpec(memory_space=pl.ANY),
         ],
         out_specs=[
@@ -295,7 +296,7 @@
         compiler_params=params,
         cost_estimate=pl.CostEstimate(flops=30_000_000_000, bytes_accessed=6_000_000, transcendentals=0),
         name="own_part",
-    )(lines, degrees, features)
+    )(lines, degrees, most, features)
 
     whole = lambda *shape: pl.BlockSpec(shape, lambda i: (0,) * len(shape))
     last_early = early // tile - 1

time: 75.1 us -> 74.8 us (level)
  no operation moved by 1% of the time
where the time goes in v6:
time: 74.8 us; the launch traced here: 74.5 us
  Pallas kernels  67.1 us (90%)
  starting transfers between devices  7.43 us (10%)
    pallas_call x1, Pallas kernels, local(): pl.pallas_call(functools.partial(layer_kernel, tile=tile, early=early, gr...  47.8 us
    pallas_call x1, Pallas kernels, local(): pl.pallas_call(functools.partial(own_kernel, tile=tile, early=early, grou...  15.4 us
    all_to_all x1, starting transfers between devices, local(): lax.all_to_all(outgoing.reshape(peers, block, width), 'node', split_axis=...  7.43 us
    pallas_call x1, Pallas kernels, local(): pl.pallas_call(functools.partial(outgoing_kernel, peers=peers, rows=rows,...  3.92 us
  transfers between devices with their start and end apart: 1, of which 0 were waited for; matrix products, arithmetic and copies ran while one was open for 0% of the time, Pallas kernels for 21%

profile of v6, /device:TPU:0, one launch (start us, length us, event | category | flops | bytes accessed | tf_op | source)
XLA Modules:
  0.0 74.5 jit_solution(17519168442007307445)
XLA Ops:
  0.0 3.9 %outgoing_rows.1 = (bf16[2176,128]{1,0:T(8,128)(2,1)}, f32[8,128]{1,0:T(8,128)}) custom-call(s32[2048]{0:T(1024)} %bitcast.14, s32[8]{0:T(128)} %bitcast.15, bf16[8192,128]{1,0:T(8,128)(2,1)} %feat_ref.5), custom_call_target="tpu_custom_call" | custom-call | tf_op jit(solution)/shard_map/outgoing_rows/pallas_call | solution.py:255
  3.9 7.4 %all-to-all-start = ((bf16[16,136,128]{2,1,0:T(8,128)(2,1)}), bf16[16,136,128]{2,1,0:T(8,128)(2,1)}, u32[]{:S(2)}, u32[]{:S(2)}) async-start(bf16[16,136,128]{2,1,0:T(8,128)(2,1)} %bitcast.11), calls=%async_computation | async-start | bytes 1114112 | tf_op jit(solution)/shard_map/all_to_all | solution.py:264
  11.4 15.4 %own_part.1 = (s32[512,256]{1,0:T(8,128)}, f8e4m3fn[8192,256]{1,0:T(32,128)(4,1)}, f32[2048,128]{1,0:T(8,128)}, f32[8,128]{1,0:T(8,128)}) custom-call(s32[2,64,8,128]{3,2,1,0:T(8,128)} %bitcast.17, s32[64,128]{1,0:T(8,128)} %bitcast.12, f32[8,128]{1,0:T(8,128)} %get-tuple-element.11.most_ref, bf16[8192,128]{1,0:T(8,128)(2,1)} %feat_ref.5), custom_call_target="tpu_custom_call" | custom-call | flops 30000001024 | bytes 6000000 | tf_op jit(solution)/shard_map/own_part/pallas_call | solution.py:267
  26.8 0.0 all-to-all-done
  26.8 47.8 %sage_layer.1 = bf16[8192,128]{1,0:T(8,128)(2,1)} custom-call(s32[512,256]{1,0:T(8,128)} %get-tuple-element.12.index_ref, s32[64,128]{1,0:T(8,128)} %bitcast.13, f32[2048,128]{1,0:T(8,128)} %get-tuple-element.13.part_ref, f32[8,128]{1,0:T(8,128)} %get-tuple-element.14.own_inverse, bf16[8192,128]{1,0:T(8,128)(2,1)} %feat_ref.5, ...), custom_call_target="tpu_custom_call" | custom-call | tf_op jit(solution)/shard_map/sage_layer/pallas_call | solution.py:303
Async XLA Ops:
  3.9 22.8 %all-to-all-start = ((bf16[16,136,128]{2,1,0:T(8,128)(2,1)}), bf16[16,136,128]{2,1,0:T(8,128)(2,1)}, u32[]{:S(2)}, u32[]{:S(2)}) async-start(bf16[16,136,128]{2,1,0:T(8,128)(2,1)} %bitcast.11), calls=%async_computation | async-start | bytes 1114112 | tf_op jit(solution)/shard_map/all_to_all | solution.py:264
